TPU v7x, 32 devices: a whole 2x2x4 slice. The times are simulated.
32 devices in a mesh: energy: 8 (over z, y), slab: 4 (over x, core).
Axes of the slice: x: 2, y: 2, z: 4, core: 2. Of those that a mesh axis runs over, the one named last changes fastest.
Arguments:
- lesser: bfloat16 [8, 4, 2, 1024, 1024], P('energy', 'slab'), may hold values from -6 to 6
- greater_diag: float32 [8, 4, 1024], P('energy', 'slab'), may hold values from -6 to 6
- dipole: bfloat16 [4, 1024, 1024], P('slab'), may hold values from -0.1875 to 0.1875
- photon_weights: float32 [8, 3], P('energy'), may hold values from 0.2 to 1
- sidebands: int32 [8], P('energy'), may hold values from 1 to 2
- phonon_lags: int32 [6], replicated, may hold values from 1 to 3
- phonon_strengths: float32 [2, 6], replicated, may hold values from 0.3 to 1.5
- slab_coupling: float32 [4, 1024], P('slab'), may hold values from 0.3 to 1
Outputs:
- lesser_self: bfloat16 [8, 4, 2, 1024, 1024], P('energy', 'slab')
- greater_phonon: float32 [8, 4, 1024], P('energy', 'slab')
All inputs are finite; a program needn't handle non-finite values.
Results may differ from a plain program's by a relative error of at most 0.0057.
Values may be sent and summed in bfloat16 or wider, within the bound.
No kernel may reach another device: no remote copies, remote signals or barrier semaphores. Data moves between devices by JAX's collectives and lax.ppermute only.
A program may use at most 64 MiB of HBM per device.

v0:
```python
import functools

import jax
import jax.numpy as jnp
from jax import lax
from jax.experimental import pallas as pl
from jax.experimental.pallas import tpu as pltpu
from jax.sharding import PartitionSpec as P

PHOT_BLOCKS = 3
CHUNKS = (((0, 0, 8),), ((1, 0, 2),), ((1, 2, 5),), ((1, 7, 1),))
MIDDLE = ((1, 0, 7),)
EIGHTHS = 8
VMEM_BYTES = 20 * 1024 * 1024
EARLY_VMEM_BYTES = 53 * 1024 * 1024
FIRST_VMEM_BYTES = 48 * 1024 * 1024

STRAIGHT = ((0, 3), (2, 5), (3, 6), (4, 1), (5, 2), (7, 4))
CROSS = ((1, 4), (3, 0), (4, 7), (6, 3))
DETOURS = ((1, 0, 4), (6, 7, 3))
EDGES = ((3, 0), (4, 7))
OTHERS = ((1, 4), (6, 3))
EDGES_BY = ((3, 2), (4, 5))
EDGES_ON = ((2, 0), (5, 7))

TO_HUBS = ((3, 1), (4, 6))
BETWEEN_HUBS = ((1, 6), (6, 1))
FROM_HUBS = (((1, 3), (6, 4)), ((1, 5), (6, 2)), ((1, 7), (6, 0)))


def shifted(block, axis, distance):
    devices = range(lax.axis_size(axis))
    return lax.ppermute(
        block, axis, [(i - distance, i) for i in devices if i - distance in devices]
    )


def any_of(own, energies):
    return functools.reduce(jnp.logical_or, [own == energy for energy in energies])


def side_weight(own, route, low, high):
    from_low = any_of(own, [target for source, target in route if source < target])
    from_high = any_of(own, [target for source, target in route if source > target])
    return jnp.where(from_low, low, jnp.where(from_high, high, 0.0))


def doubled(block, axis, step):
    other = lax.ppermute(block, axis, [(i, i ^ step) for i in range(lax.axis_size(axis))])
    upper = (lax.axis_index(axis) & step) != 0
    return jnp.concatenate(
        [jnp.where(upper, other, block), jnp.where(upper, block, other)], axis=0
    )


def diagonals_body(tile, lesser_ref, greater_ref, out_ref, tiles, arrived):
    count = tiles.shape[0]
    copies = [
        pltpu.make_async_copy(
            lesser_ref.at[0, 0, 1, pl.ds(n * tile, tile), pl.ds(n * tile, tile)],
            tiles.at[n],
            arrived.at[n],
        )
        for n in range(count)
    ]
    for copy in copies:
        copy.start()
    row = lax.broadcasted_iota(jnp.int32, (tile, tile), 0)
    col = lax.broadcasted_iota(jnp.int32, (tile, tile), 1)
    out_ref[0, 1:2] = greater_ref[0]
    for n, copy in enumerate(copies):
        copy.wait()
        block = jnp.where(row == col, tiles[n].astype(jnp.float32), 0.0)
        out_ref[0, 0:1, n * tile : (n + 1) * tile] = jnp.sum(block, axis=0, keepdims=True)


def diagonals_of(lesser, greater_diag):
    width = lesser.shape[-1]
    tile = 128
    return pl.pallas_call(
        functools.partial(diagonals_body, tile),
        in_specs=[
            pl.BlockSpec(memory_space=pltpu.HBM),
            pl.BlockSpec(memory_space=pltpu.VMEM),
        ],
        out_specs=pl.BlockSpec(memory_space=pltpu.VMEM),
        out_shape=jax.ShapeDtypeStruct((1, 2, width), jnp.float32),
        scratch_shapes=[
            pltpu.VMEM((width // tile, tile, tile), lesser.dtype),
            pltpu.SemaphoreType.DMA((width // tile,)),
        ],
        compiler_params=pltpu.CompilerParams(vmem_limit_bytes=EARLY_VMEM_BYTES),
        name="diagonals",
    )(lesser, greater_diag)


def lag_kernel(rows, cols, phonon_lags, first, second):
    offset = cols[None, :] - rows[:, None]
    upward = (offset[None, :, :] == phonon_lags[:, None, None]).astype(jnp.float32)
    downward = (offset[None, :, :] == -phonon_lags[:, None, None]).astype(jnp.float32)
    return jnp.sum(first[:, None, None] * upward + second[:, None, None] * downward, axis=0)


def lag_sums(rows, everyone, phonon_lags, strengths):
    cols = jnp.arange(everyone.shape[0], dtype=jnp.int32)
    k_less = lag_kernel(rows, cols, phonon_lags, strengths[0], strengths[1])
    k_great = lag_kernel(rows, cols, phonon_lags, strengths[1], strengths[0])
    kernels = jnp.stack([k_less, k_great], axis=-1)
    return jnp.sum(kernels[..., None] * everyone[None], axis=1)


def left_body(chunk, streamed, lesser_ref, dipole_ref, left_ref, *scratch):
    width = left_ref.shape[0]
    unit, rows = width // EIGHTHS, width // 4
    starts = range(0, width, rows)
    if streamed:
        blocks, arrived = scratch
        copies = [
            pltpu.make_async_copy(
                lesser_ref.at[0, 0, chunk[0][0], pl.ds(i, rows)], blocks.at[pl.ds(i, rows)], sem
            )
            for i, sem in zip(starts, [arrived.at[n] for n in range(len(starts))])
        ]
        for copy in copies:
            copy.start()
    at = 0
    for part, first, eighths in chunk:
        cols = eighths * unit
        for n, i in enumerate(starts):
            if streamed:
                copies[n].wait()
                block = blocks[i : i + rows]
            else:
                block = lesser_ref[0, 0, part, i : i + rows]
            left_ref[i : i + rows, at : at + cols] = lax.dot_general(
                block,
                dipole_ref[0, first * unit : first * unit + cols],
                (((1,), (1,)), ((), ())),
                preferred_element_type=jnp.float32,
            ).astype(left_ref.dtype)
        at += cols


def left_of(lesser, dipole, chunk, streamed=False):
    width = lesser.shape[-1]
    cols = width // EIGHTHS * sum(eighths for _, _, eighths in chunk)
    scratch = [pltpu.VMEM((width, width), lesser.dtype), pltpu.SemaphoreType.DMA((4,))]
    return pl.pallas_call(
        functools.partial(left_body, chunk, streamed),
        in_specs=[
            pl.BlockSpec(memory_space=pl.ANY if streamed else pltpu.VMEM),
            pl.BlockSpec(memory_space=pltpu.VMEM),
        ],
        out_specs=pl.BlockSpec(memory_space=pltpu.VMEM),
        out_shape=jax.ShapeDtypeStruct((width, cols), lesser.dtype),
        scratch_shapes=scratch if streamed else [],
        compiler_params=pltpu.CompilerParams(
            vmem_limit_bytes=FIRST_VMEM_BYTES if streamed else VMEM_BYTES
        ),
        name="left",
    )(lesser, dipole)


def either_body(flag_ref, yes_ref, no_ref, out_ref):
    height = out_ref.shape[0]
    rows = height // 16

    def copied_from(ref):
        @pl.loop(0, height // rows)
        def _(i):
            at = pl.ds(pl.multiple_of(i * rows, rows), rows)
            out_ref[at] = ref[at]

    pl.when(flag_ref[0] != 0)(lambda: copied_from(yes_ref))
    pl.when(flag_ref[0] == 0)(lambda: copied_from(no_ref))


def either_of(flag, yes, no):
    return pl.pallas_call(
        either_body,
        in_specs=[
            pl.BlockSpec(memory_space=pltpu.SMEM),
            pl.BlockSpec(memory_space=pltpu.VMEM),
            pl.BlockSpec(memory_space=pltpu.VMEM),
        ],
        out_specs=pl.BlockSpec(memory_space=pltpu.VMEM),
        out_shape=jax.ShapeDtypeStruct(yes.shape, yes.dtype),
        compiler_params=pltpu.CompilerParams(vmem_limit_bytes=VMEM_BYTES),
        name="either",
    )(flag.astype(jnp.int32).reshape(1), yes, no)


def held_body(block_ref, out_ref):
    out_ref[...] = block_ref[...]


def held_of(block, flops):
    return pl.pallas_call(
        held_body,
        in_specs=[pl.BlockSpec(memory_space=pltpu.VMEM)],
        out_specs=pl.BlockSpec(memory_space=pltpu.VMEM),
        out_shape=jax.ShapeDtypeStruct(block.shape, block.dtype),
        cost_estimate=pl.CostEstimate(flops=flops, bytes_accessed=0, transcendentals=0),
        compiler_params=pltpu.CompilerParams(vmem_limit_bytes=VMEM_BYTES),
        name="held",
    )(block)


def pieces_of(chunk):
    pieces, place = [], 0
    for part, first, eighths in chunk:
        for at in range(first, first + eighths, 2):
            size = min(2, first + eighths - at)
            pieces.append((part, at, place, size))
            place += size
    return pieces


def photon_body(segments, factors_ref, dipole_ref, phonon_ref, *refs):
    out_ref, results, sent = refs[-3:]
    copies = []
    for chunk, skips in segments:
        own_ref, *sides = refs[: 1 + len(skips)]
        refs = refs[1 + len(skips) :]
        width = own_ref.shape[0]
        unit = width // EIGHTHS
        factors = [factors_ref[n] for n in range(2 + len(skips))]
        for part, at, place, size in pieces_of(chunk):
            at, place, cols = at * unit, place * unit, size * unit

            def piece(ref, skip=0):
                start = skip * unit + place
                return ref[:, start : start + cols].astype(jnp.float32)

            side = factors[2] * piece(sides[0], skips[0])
            for factor, ref, skip in zip(factors[3:], sides[1:], skips[1:]):
                side += factor * piece(ref, skip)
            mixed = (factors[0] * piece(own_ref) + factors[1] * side).astype(jnp.bfloat16)
            photon = jnp.dot(dipole_ref[0], mixed, preferred_element_type=jnp.float32)
            if part == 1:
                row = lax.broadcasted_iota(jnp.int32, photon.shape, 0)
                col = lax.broadcasted_iota(jnp.int32, photon.shape, 1) + at
                photon += jnp.where(row == col, phonon_ref[:, at : at + cols], 0.0)
            k = len(copies)
            results[k, :, :cols] = photon.astype(results.dtype)
            copies.append(
                pltpu.make_async_copy(
                    results.at[k, :, pl.ds(0, cols)],
                    out_ref.at[0, 0, part, :, pl.ds(at, cols)],
                    sent.at[k],
                )
            )
            copies[-1].start()
    for copy in copies:
        copy.wait()


def photon_of(segments, factors, dipole, phonon, out):
    width = dipole.shape[-1]
    n_pieces = sum(len(pieces_of(chunk)) for chunk, _, _ in segments)
    operands = [factors, dipole, phonon]
    for _, own, sides in segments:
        operands += [own, *(block for block, _ in sides)]
    layout = [(chunk, [skip for _, skip in sides]) for chunk, _, sides in segments]
    in_specs = [pl.BlockSpec(memory_space=pltpu.SMEM)]
    in_specs += [pl.BlockSpec(memory_space=pltpu.VMEM)] * (len(operands) - 1)
    aliases = {}
    if out is not None:
        aliases = {len(operands): 0}
        operands.append(out)
        in_specs.append(pl.BlockSpec(memory_space=pl.ANY))
    return pl.pallas_call(
        functools.partial(photon_body, layout),
        in_specs=in_specs,
        out_specs=pl.BlockSpec(memory_space=pl.ANY),
        out_shape=jax.ShapeDtypeStruct((1, 1, 2, width, width), jnp.bfloat16),
        scratch_shapes=[
            pltpu.VMEM((n_pieces, width, 2 * width // EIGHTHS), jnp.bfloat16),
            pltpu.SemaphoreType.DMA((n_pieces,)),
        ],
        input_output_aliases=aliases,
        compiler_params=pltpu.CompilerParams(vmem_limit_bytes=VMEM_BYTES),
        name="photon",
    )(*operands)


def on_device(
    lesser,
    greater_diag,
    dipole,
    photon_weights,
    sidebands,
    phonon_lags,
    phonon_strengths,
    slab_coupling,
):
    width = lesser.shape[-1]
    count = lax.axis_size("energy")
    own = lax.axis_index("energy")
    everyone = doubled(diagonals_of(lesser, greater_diag), "energy", 1)
    left = [left_of(lesser, dipole, CHUNKS[0], streamed=True)]
    left += [left_of(lesser, dipole, chunk) for chunk in CHUNKS[1:]]
    everyone, left[0] = lax.optimization_barrier((everyone, left[0]))
    weight_0, weight_low, weight_high = photon_weights[0]
    flag = sidebands[0].astype(jnp.float32)
    if count == 8:
        first, second = {}, {}
        hops = tuple((source, by) for source, by, _ in DETOURS)
        second_hops = tuple((by, target) for _, by, target in DETOURS)
        first[0] = lax.ppermute(left[0], "energy", STRAIGHT + hops)

        is_low = own < count // 2
        for route in (TO_HUBS, BETWEEN_HUBS):
            other = lax.ppermute(everyone, "energy", route)
            everyone = jnp.concatenate(
                [jnp.where(is_low, everyone, other), jnp.where(is_low, other, everyone)], axis=0
            )
        hubs = [hub for hub, _ in BETWEEN_HUBS]
        to = [[own] + [dict(route)[hub] for route in FROM_HUBS] for hub in hubs]
        rows = [jnp.where(is_low, low, high) for low, high in zip(*to)]
        everyone, left[1] = lax.optimization_barrier((everyone, left[1]))
        first[1] = lax.ppermute(left[1], "energy", STRAIGHT)
        sums = lag_sums(jnp.stack(rows), everyone, phonon_lags, phonon_strengths)
        correlated = jnp.where(any_of(own, hubs), sums[0], 0.0)
        for n, route in enumerate(FROM_HUBS):
            correlated += lax.ppermute(sums[n + 1], "energy", route)

        middle = left_of(lesser, dipole, MIDDLE)
        first[0], correlated, *left, middle = lax.optimization_barrier(
            (first[0], correlated, *left, middle)
        )
        relays = any_of(own, [by for by, _ in second_hops])
        onward = either_of(relays, first[0], left[0])
        second[0] = lax.ppermute(onward, "energy", EDGES + second_hops)
        crossed = lax.ppermute(middle, "energy", CROSS)
        first[2] = lax.ppermute(left[2], "energy", STRAIGHT)
        by = lax.ppermute(left[3], "energy", EDGES_BY)
        first[1] = held_of(first[1], 4000000000)
        first[1], left[3], by = lax.optimization_barrier((first[1], left[3], by))
        edge = lax.ppermute(by, "energy", EDGES_ON)
        second[3] = lax.ppermute(left[3], "energy", OTHERS)
        first[3] = lax.ppermute(left[3], "energy", STRAIGHT)
        weights = [
            side_weight(own, STRAIGHT, weight_low, weight_high),
            side_weight(own, CROSS, weight_low, weight_high),
        ]
    else:
        step = 2
        while step < count:
            everyone = doubled(everyone, "energy", step)
            step *= 2
        correlated = lag_sums(own[None], everyone, phonon_lags, phonon_strengths)[0]
        first = [shifted(block, "energy", PHOT_BLOCKS) for block in left]
        second = [shifted(block, "energy", -PHOT_BLOCKS) for block in left]
        weights = [weight_low, weight_high]
    factors = jnp.stack([weight_0, flag, *weights, weights[1]])
    if count == 8:
        sides = [
            [(first[0], 0), (second[0], 0)],
            [(first[1], 0), (crossed, 0)],
            [(first[2], 0), (crossed, 2)],
            [(first[3], 0), (second[3], 0), (edge, 0)],
        ]
    else:
        sides = [[(low, 0), (high, 0)] for low, high in zip(first, second)]

    correlated = held_of(correlated, 17000000000)
    below = shifted(slab_coupling * correlated, "slab", 1)
    above = shifted(correlated, "slab", -1)
    phon_less, phon_great = correlated + below + slab_coupling * above

    out = None
    for together in ((0,), (1, 2), (3,)):
        segments = [(CHUNKS[n], left[n], sides[n]) for n in together]
        out = photon_of(segments, factors, dipole, phon_less[None], out)
    return out, phon_great[None, None]


def solution(mesh):
    return jax.shard_map(
        on_device,
        mesh=mesh,
        in_specs=(
            P("energy", "slab", None, None, None),
            P("energy", "slab", None),
            P("slab", None, None),
            P("energy", None),
            P("energy"),
            P(),
            P(),
            P("slab", None),
        ),
        out_specs=(P("energy", "slab", None, None, None), P("energy", "slab", None)),
        check_vma=False,
    )
```

profile of v0, /device:TPU:0, one launch (start us, length us, event | category | flops | bytes accessed | tf_op | source)
XLA Modules:
  0.0 157.6 jit_solution(12732900500413984085)
XLA Ops:
  0.6 0.0 copy-start.2
  0.6 0.0 copy-start.11
  0.6 0.8 copy-done.11
  1.5 1.0 diagonals.1
  2.5 3.0 %collective-permute-start = (f32[1,2,1024]{2,1,0:T(2,128)S(1)}, f32[1,2,1024]{2,1,0:T(2,128)S(1)}, u32[]{:S(2)}, u32[]{:S(2)}) collective-permute-start(f32[1,2,1024]{2,1,0:T(2,128)S(1)} %diagonals.1), channel_id=1, source_target_pairs={{0,4},{4,0},{8,12},{12,8},{16,20},{20,16},{24,28},{28,24},{1,5},{5... | collective-permute-start | bytes 24584 | tf_op jit(solution)/shard_map/ppermute | solution.py:49
  5.6 4.1 %left.5.no_ref.refs_0_ = bf16[1024,1024]{1,0:T(8,128)(2,1)S(1)} custom-call(bf16[1,1,2,1024,1024]{4,3,2,1,0:T(8,128)(2,1)} %lesser_ref.11, bf16[1,1024,1024]{2,1,0:T(8,128)(2,1)S(1)} %copy-done.2), custom_call_target="tpu_custom_call" | custom-call | tf_op jit(solution)/shard_map/left/pallas_call | solution.py:148
  9.6 0.0 copy-start.3
  9.6 1.3 copy-done.3
  11.0 0.0 collective-permute-done
  11.0 1.6 collective-permute-start.1
  12.6 0.1 pad_add_fusion
  12.7 0.1 iota_subtract_fusion
  12.7 0.7 collective-permute-start.2
  13.4 0.1 fusion.1
  13.5 0.0 collective-permute-done.2
  13.6 0.7 collective-permute-start.3
  14.2 0.0 copy-start
  14.2 2.2 %copy-done = bf16[1,1,2,1024,1024]{4,3,2,1,0:T(8,128)(2,1)S(1)} copy-done((bf16[1,1,2,1024,1024]{4,3,2,1,0:T(8,128)(2,1)S(1)}, bf16[1,1,2,1024,1024]{4,3,2,1,0:T(8,128)(2,1)}, u32[]{:S(2)}) %copy-start) | copy-done | bytes 4194328
  16.4 0.7 left.6.refs_0_
  17.2 0.8 copy-done.5
  18.0 0.0 collective-permute-done.3
  18.1 0.2 multiply_reduce_fusion
  18.3 0.7 collective-permute-start.4
  18.9 0.7 collective-permute-start.5
  19.6 1.3 collective-permute-start.6
  20.9 0.6 fusion.8
  21.5 2.2 %copy-done.1 = bf16[1,1,2,1024,1024]{4,3,2,1,0:T(8,128)(2,1)S(1)} copy-done((bf16[1,1,2,1024,1024]{4,3,2,1,0:T(8,128)(2,1)S(1)}, bf16[1,1,2,1024,1024]{4,3,2,1,0:T(8,128)(2,1)}, u32[]{:S(2)}) %copy-start.1) | copy-done | bytes 4194328
  23.7 2.4 %left.9 = bf16[1024,896]{1,0:T(8,128)(2,1)S(1)} custom-call(bf16[1,1,2,1024,1024]{4,3,2,1,0:T(8,128)(2,1)S(1)} %copy-done.1, bf16[1,1024,1024]{2,1,0:T(8,128)(2,1)S(1)} %copy-done.2), custom_call_target="tpu_custom_call" | custom-call | tf_op jit(solution)/shard_map/left/pallas_call | solution.py:148
  26.1 1.2 copy-done.7
  27.3 1.8 %left.7.refs_3_ = bf16[1024,640]{1,0:T(8,128)(2,1)S(1)} custom-call(bf16[1,1,2,1024,1024]{4,3,2,1,0:T(8,128)(2,1)S(1)} %copy-done.1, bf16[1,1024,1024]{2,1,0:T(8,128)(2,1)S(1)} %copy-done.2), custom_call_target="tpu_custom_call" | custom-call | tf_op jit(solution)/shard_map/left/pallas_call | solution.py:148
  29.2 0.7 left.8.refs_0_
  29.9 0.7 copy-done.9
  33.6 0.8 stack.37.factors_ref
  34.4 7.4 %collective-permute-start.9 = (bf16[1024,256]{1,0:T(8,128)(2,1)}, bf16[1024,256]{1,0:T(8,128)(2,1)S(1)}, u32[]{:S(2)}, u32[]{:S(2)}) collective-permute-start(bf16[1024,256]{1,0:T(8,128)(2,1)} %copy-done.5), channel_id=1, source_target_pairs={{0,12},{8,20},{12,24},{16,4},{20,8},{28,16},{1,13},{9,21},{13,25},... | collective-permute-start | bytes 1572872 | tf_op jit(solution)/shard_map/ppermute | solution.py:322
  41.8 0.0 collective-permute-done.4
  41.9 0.0 collective-permute-done.5
  41.9 0.0 collective-permute-done.6
  41.9 17.1 %collective-permute-done.1.yes_ref.refs_1_ = bf16[1024,1024]{1,0:T(8,128)(2,1)} collective-permute-done((bf16[1024,1024]{1,0:T(8,128)(2,1)}, bf16[1024,1024]{1,0:T(8,128)(2,1)}, u32[]{:S(2)}, u32[]{:S(2)}) %collective-permute-start.1) | collective-permute-done | bytes 2097184 | tf_op jit(solution)/shard_map/ppermute | solution.py:310
  59.0 1.6 %copy-done.4 = bf16[1024,1024]{1,0:T(8,128)(2,1)S(1)} copy-done((bf16[1024,1024]{1,0:T(8,128)(2,1)S(1)}, bf16[1024,1024]{1,0:T(8,128)(2,1)}, u32[]{:S(2)}) %copy-start.4) | copy-done | bytes 2097176
  60.6 1.9 %either.1 = bf16[1024,1024]{1,0:T(8,128)(2,1)S(1)} custom-call(s32[1]{0:T(128)} %bitcast.18.flag_ref, bf16[1024,1024]{1,0:T(8,128)(2,1)} %collective-permute-done.1.yes_ref.refs_1_, bf16[1024,1024]{1,0:T(8,128)(2,1)S(1)} %copy-done.4), custom_call_target="tpu_custom_call" | custom-call | tf_op jit(solution)/shard_map/either/pallas_call | solution.py:179
  62.5 0.0 copy-start.12
  62.5 6.4 %collective-permute-start.16 = (bf16[1024,1024]{1,0:T(8,128)(2,1)S(1)}, bf16[1024,1024]{1,0:T(8,128)(2,1)S(1)}, u32[]{:S(2)}, u32[]{:S(2)}) collective-permute-start(bf16[1024,1024]{1,0:T(8,128)(2,1)S(1)} %either.1), channel_id=1, source_target_pairs={{12,0},{16,28},{0,16},{28,12},{13,1},{17,29},{1,17},{29,13},{14,2}... | collective-permute-start | bytes 6291464 | tf_op jit(solution)/shard_map/ppermute | solution.py:334
  68.9 1.3 collective-permute-start.14
  70.2 0.7 collective-permute-start.10
  70.9 6.2 %collective-permute-start.15 = (bf16[1024,640]{1,0:T(8,128)(2,1)S(1)}, bf16[1024,640]{1,0:T(8,128)(2,1)S(1)}, u32[]{:S(2)}, u32[]{:S(2)}) collective-permute-start(bf16[1024,640]{1,0:T(8,128)(2,1)S(1)} %left.7.refs_3_), channel_id=1, source_target_pairs={{0,12},{8,20},{12,24},{16,4},{20,8},{28,16},{1,13},{9,21},{13,25},... | collective-permute-start | bytes 3932168 | tf_op jit(solution)/shard_map/ppermute | solution.py:336
  77.1 0.0 collective-permute-done.9.block_ref
  77.1 1.3 collective-permute-start.8
  78.4 0.0 collective-permute-done.10
  78.4 3.0 %collective-permute-start.7 = (f32[2,1024]{1,0:T(2,128)S(1)}, f32[2,1024]{1,0:T(2,128)S(1)}, u32[]{:S(2)}, u32[]{:S(2)}) collective-permute-start(f32[2,1024]{1,0:T(2,128)S(1)} %broadcast_multiply_fusion), channel_id=1, source_target_pairs={{0,1},{1,2},{2,3},{4,5},{5,6},{6,7},{8,9},{9,10},{10,11},{12,13},{... | collective-permute-start | bytes 24584 | tf_op jit(solution)/shard_map/ppermute | solution.py:33
  81.5 0.8 collective-permute-done.7
  82.2 44.6 %collective-permute-start.11 = (bf16[1024,128]{1,0:T(8,128)(2,1)S(1)}, bf16[1024,128]{1,0:T(8,128)(2,1)S(1)}, u32[]{:S(2)}, u32[]{:S(2)}) collective-permute-start(bf16[1024,128]{1,0:T(8,128)(2,1)S(1)} %copy-done.10), channel_id=1, source_target_pairs={{0,12},{8,20},{12,24},{16,4},{20,8},{28,16},{1,13},{9,21},{13,25},... | collective-permute-start | bytes 786440 | tf_op jit(solution)/shard_map/ppermute | solution.py:342
  126.8 0.0 collective-permute-done.8
  126.8 0.7 collective-permute-start.12
  127.5 0.0 collective-permute-done.16.refs_2_
  127.5 1.5 collective-permute-start.13
  129.0 0.6 slice_bitcast_fusion.3
  129.6 5.2 %photon.3.refs_6_ = bf16[1,1,2,1024,1024]{4,3,2,1,0:T(8,128)(2,1)} custom-call(f32[5]{0:T(128)S(1)} %stack.37.factors_ref, bf16[1,1024,1024]{2,1,0:T(8,128)(2,1)S(1)} %copy-done.2, f32[1,1024]{1,0:T(1,128)S(1)} %get-tuple-element.42.phonon_ref, bf16[1024,1024]{1,0:T(8,128)(2,1)S(1)} %copy-done.4, bf16[1024,1024]{1,0:T(8,128)(2,1)} %collective-permute-done.1.yes_ref.refs_1_, ...), custom_call_target="tpu_custom_call" | custom-call | tf_op jit(solution)/shard_map/photon/pallas_call | solution.py:272
  134.9 13.9 %collective-permute-done.15.refs_4_ = bf16[1024,640]{1,0:T(8,128)(2,1)S(1)} collective-permute-done((bf16[1024,640]{1,0:T(8,128)(2,1)S(1)}, bf16[1024,640]{1,0:T(8,128)(2,1)S(1)}, u32[]{:S(2)}, u32[]{:S(2)}) %collective-permute-start.15) | collective-permute-done | bytes 1310752 | tf_op jit(solution)/shard_map/ppermute | solution.py:336
  148.7 2.6 %collective-permute-done.14.refs_2_.refs_5_ = bf16[1024,896]{1,0:T(8,128)(2,1)S(1)} collective-permute-done((bf16[1024,896]{1,0:T(8,128)(2,1)S(1)}, bf16[1024,896]{1,0:T(8,128)(2,1)S(1)}, u32[]{:S(2)}, u32[]{:S(2)}) %collective-permute-start.14) | collective-permute-done | bytes 1835040 | tf_op jit(solution)/shard_map/ppermute | solution.py:335
  151.3 4.0 %photon.4.refs_4_ = bf16[1,1,2,1024,1024]{4,3,2,1,0:T(8,128)(2,1)} custom-call(f32[5]{0:T(128)S(1)} %stack.37.factors_ref, bf16[1,1024,1024]{2,1,0:T(8,128)(2,1)S(1)} %copy-done.2, f32[1,1024]{1,0:T(1,128)S(1)} %get-tuple-element.42.phonon_ref, bf16[1024,256]{1,0:T(8,128)(2,1)S(1)} %copy-done.6, ...), custom_call_target="tpu_custom_call", output_to_operand_aliasing={{}: (9, {})} | custom-call | tf_op jit(solution)/shard_map/photon/pallas_call | solution.py:272
  155.3 0.0 collective-permute-done.11.refs_1_
  155.3 0.0 collective-permute-done.12.refs_2_
  155.3 0.0 collective-permute-done.13.refs_3_
  155.3 2.1 %photon.5 = bf16[1,1,2,1024,1024]{4,3,2,1,0:T(8,128)(2,1)} custom-call(f32[5]{0:T(128)S(1)} %stack.37.factors_ref, bf16[1,1024,1024]{2,1,0:T(8,128)(2,1)S(1)} %copy-done.2, f32[1,1024]{1,0:T(1,128)S(1)} %get-tuple-element.42.phonon_ref, bf16[1024,128]{1,0:T(8,128)(2,1)S(1)} %copy-done.10, ...), custom_call_target="tpu_custom_call", output_to_operand_aliasing={{}: (7, {})} | custom-call | tf_op jit(solution)/shard_map/photon/pallas_call | solution.py:272
  (36 shorter events, 0.3 us)
Async XLA Ops:
  0.6 4.9 %copy-start.2 = (bf16[1,1024,1024]{2,1,0:T(8,128)(2,1)S(1)}, bf16[1,1024,1024]{2,1,0:T(8,128)(2,1)}, u32[]{:S(2)}) copy-start(bf16[1,1024,1024]{2,1,0:T(8,128)(2,1)} %dipole_ref.15) | copy-start | bytes 6291460
  0.6 0.8 copy-start.11
  2.5 8.4 %collective-permute-start = (f32[1,2,1024]{2,1,0:T(2,128)S(1)}, f32[1,2,1024]{2,1,0:T(2,128)S(1)}, u32[]{:S(2)}, u32[]{:S(2)}) collective-permute-start(f32[1,2,1024]{2,1,0:T(2,128)S(1)} %diagonals.1), channel_id=1, source_target_pairs={{0,4},{4,0},{8,12},{12,8},{16,20},{20,16},{24,28},{28,24},{1,5},{5... | collective-permute-start | bytes 24584 | tf_op jit(solution)/shard_map/ppermute | solution.py:49
  5.6 5.4 %copy-start.15 = (s32[6]{0:T(128)S(1)}, s32[6]{0:T(128)}, u32[]{:S(2)}) copy-start(s32[6]{0:T(128)} %param.13) | copy-start | bytes 76
  5.6 7.1 %copy-start.14 = (f32[2,6]{1,0:T(2,128)S(1)}, f32[2,6]{1,0:T(2,128)}, u32[]{:S(2)}) copy-start(f32[2,6]{1,0:T(2,128)} %param.14) | copy-start | bytes 148
  9.6 1.3 copy-start.3
  11.0 48.0 %collective-permute-start.1 = (bf16[1024,1024]{1,0:T(8,128)(2,1)}, bf16[1024,1024]{1,0:T(8,128)(2,1)}, u32[]{:S(2)}, u32[]{:S(2)}) collective-permute-start(bf16[1024,1024]{1,0:T(8,128)(2,1)} %copy-done.3), channel_id=1, source_target_pairs={{0,12},{8,20},{12,24},{16,4},{20,8},{28,16},{4,0},{24,28},{1,13},{... | collective-permute-start | bytes 6291464 | tf_op jit(solution)/shard_map/ppermute | solution.py:310
  12.7 0.8 collective-permute-start.2
  13.6 4.4 %collective-permute-start.3 = (f32[4,2,1024]{2,1,0:T(2,128)S(1)}, f32[4,2,1024]{2,1,0:T(2,128)S(1)}, u32[]{:S(2)}, u32[]{:S(2)}) collective-permute-start(f32[4,2,1024]{2,1,0:T(2,128)S(1)} %pad_maximum_fusion.1), channel_id=1, source_target_pairs={{4,24},{24,4},{5,25},{25,5},{6,26},{26,6},{7,27},{27,7}} | collective-permute-start | bytes 98312 | tf_op jit(solution)/shard_map/ppermute | solution.py:314
  14.2 2.2 %copy-start = (bf16[1,1,2,1024,1024]{4,3,2,1,0:T(8,128)(2,1)S(1)}, bf16[1,1,2,1024,1024]{4,3,2,1,0:T(8,128)(2,1)}, u32[]{:S(2)}) copy-start(bf16[1,1,2,1024,1024]{4,3,2,1,0:T(8,128)(2,1)} %lesser_ref.11) | copy-start | bytes 12582916
  16.4 4.5 %copy-start.13 = (f32[1,3]{1,0:T(1,128)S(1)}, f32[1,3]{1,0:T(1,128)}, u32[]{:S(2)}) copy-start(f32[1,3]{1,0:T(1,128)} %param.11) | copy-start | bytes 40
  17.2 0.8 copy-start.5
  18.3 23.6 %collective-permute-start.4 = (f32[2,1024]{1,0:T(2,128)S(1)}, f32[2,1024]{1,0:T(2,128)S(1)}, u32[]{:S(2)}, u32[]{:S(2)}) collective-permute-start(f32[2,1024]{1,0:T(2,128)S(1)} %get-tuple-element.34), channel_id=1, source_target_pairs={{4,12},{24,16},{5,13},{25,17},{6,14},{26,18},{7,15},{27,19}} | collective-permute-start | bytes 24584 | tf_op jit(solution)/shard_map/ppermute | solution.py:326
  18.9 22.9 %collective-permute-start.5 = (f32[2,1024]{1,0:T(2,128)S(1)}, f32[2,1024]{1,0:T(2,128)S(1)}, u32[]{:S(2)}, u32[]{:S(2)}) collective-permute-start(f32[2,1024]{1,0:T(2,128)S(1)} %get-tuple-element.36), channel_id=1, source_target_pairs={{4,20},{24,8},{5,21},{25,9},{6,22},{26,10},{7,23},{27,11}} | collective-permute-start | bytes 24584 | tf_op jit(solution)/shard_map/ppermute | solution.py:326
  19.6 22.3 %collective-permute-start.6 = (f32[2,1024]{1,0:T(2,128)S(1)}, f32[2,1024]{1,0:T(2,128)S(1)}, u32[]{:S(2)}, u32[]{:S(2)}) collective-permute-start(f32[2,1024]{1,0:T(2,128)S(1)} %get-tuple-element.35), channel_id=1, source_target_pairs={{4,28},{24,0},{5,29},{25,1},{6,30},{26,2},{7,31},{27,3}} | collective-permute-start | bytes 24584 | tf_op jit(solution)/shard_map/ppermute | solution.py:326
  21.5 2.2 %copy-start.1 = (bf16[1,1,2,1024,1024]{4,3,2,1,0:T(8,128)(2,1)S(1)}, bf16[1,1,2,1024,1024]{4,3,2,1,0:T(8,128)(2,1)}, u32[]{:S(2)}) copy-start(bf16[1,1,2,1024,1024]{4,3,2,1,0:T(8,128)(2,1)} %lesser_ref.11) | copy-start | bytes 12582916
  26.1 1.3 copy-start.7
  29.9 0.7 copy-start.9
  34.4 42.7 %collective-permute-start.9 = (bf16[1024,256]{1,0:T(8,128)(2,1)}, bf16[1024,256]{1,0:T(8,128)(2,1)S(1)}, u32[]{:S(2)}, u32[]{:S(2)}) collective-permute-start(bf16[1024,256]{1,0:T(8,128)(2,1)} %copy-done.5), channel_id=1, source_target_pairs={{0,12},{8,20},{12,24},{16,4},{20,8},{28,16},{1,13},{9,21},{13,25},... | collective-permute-start | bytes 1572872 | tf_op jit(solution)/shard_map/ppermute | solution.py:322
  59.0 1.6 %copy-start.4 = (bf16[1024,1024]{1,0:T(8,128)(2,1)S(1)}, bf16[1024,1024]{1,0:T(8,128)(2,1)}, u32[]{:S(2)}) copy-start(bf16[1024,1024]{1,0:T(8,128)(2,1)} %copy-done.3) | copy-start | bytes 6291460
  60.6 8.3 %copy-start.8 = (bf16[1024,896]{1,0:T(8,128)(2,1)S(1)}, bf16[1024,896]{1,0:T(8,128)(2,1)}, u32[]{:S(2)}) copy-start(bf16[1024,896]{1,0:T(8,128)(2,1)} %copy-done.7) | copy-start | bytes 5505028
  60.6 9.6 %copy-start.10 = (bf16[1024,128]{1,0:T(8,128)(2,1)S(1)}, bf16[1024,128]{1,0:T(8,128)(2,1)}, u32[]{:S(2)}) copy-start(bf16[1024,128]{1,0:T(8,128)(2,1)} %copy-done.9) | copy-start | bytes 786436
  62.5 14.6 %copy-start.12 = (f32[1,1024]{1,0:T(1,128)S(1)}, f32[1,1024]{1,0:T(1,128)}, u32[]{:S(2)}) copy-start(f32[1,1024]{1,0:T(1,128)} %param.15) | copy-start | bytes 12292
  62.5 65.0 %collective-permute-start.16 = (bf16[1024,1024]{1,0:T(8,128)(2,1)S(1)}, bf16[1024,1024]{1,0:T(8,128)(2,1)S(1)}, u32[]{:S(2)}, u32[]{:S(2)}) collective-permute-start(bf16[1024,1024]{1,0:T(8,128)(2,1)S(1)} %either.1), channel_id=1, source_target_pairs={{12,0},{16,28},{0,16},{28,12},{13,1},{17,29},{1,17},{29,13},{14,2}... | collective-permute-start | bytes 6291464 | tf_op jit(solution)/shard_map/ppermute | solution.py:334
  68.9 82.4 %collective-permute-start.14 = (bf16[1024,896]{1,0:T(8,128)(2,1)S(1)}, bf16[1024,896]{1,0:T(8,128)(2,1)S(1)}, u32[]{:S(2)}, u32[]{:S(2)}) collective-permute-start(bf16[1024,896]{1,0:T(8,128)(2,1)S(1)} %copy-done.8), channel_id=1, source_target_pairs={{4,16},{12,0},{16,28},{24,12},{5,17},{13,1},{17,29},{25,13},{6,18}... | collective-permute-start | bytes 5505032 | tf_op jit(solution)/shard_map/ppermute | solution.py:335
  70.2 8.2 %collective-permute-start.10 = (bf16[1024,128]{1,0:T(8,128)(2,1)S(1)}, bf16[1024,128]{1,0:T(8,128)(2,1)S(1)}, u32[]{:S(2)}, u32[]{:S(2)}) collective-permute-start(bf16[1024,128]{1,0:T(8,128)(2,1)S(1)} %copy-done.10), channel_id=1, source_target_pairs={{12,8},{16,20},{13,9},{17,21},{14,10},{18,22},{15,11},{19,23}} | collective-permute-start | bytes 786440 | tf_op jit(solution)/shard_map/ppermute | solution.py:337
  70.9 77.9 %collective-permute-start.15 = (bf16[1024,640]{1,0:T(8,128)(2,1)S(1)}, bf16[1024,640]{1,0:T(8,128)(2,1)S(1)}, u32[]{:S(2)}, u32[]{:S(2)}) collective-permute-start(bf16[1024,640]{1,0:T(8,128)(2,1)S(1)} %left.7.refs_3_), channel_id=1, source_target_pairs={{0,12},{8,20},{12,24},{16,4},{20,8},{28,16},{1,13},{9,21},{13,25},... | collective-permute-start | bytes 3932168 | tf_op jit(solution)/shard_map/ppermute | solution.py:336
  77.1 49.7 %collective-permute-start.8 = (f32[2,1024]{1,0:T(2,128)S(1)}, f32[2,1024]{1,0:T(2,128)S(1)}, u32[]{:S(2)}, u32[]{:S(2)}) collective-permute-start(f32[2,1024]{1,0:T(2,128)S(1)} %held.2), channel_id=1, source_target_pairs={{1,0},{2,1},{3,2},{5,4},{6,5},{7,6},{9,8},{10,9},{11,10},{13,12},{... | collective-permute-start | bytes 24584 | tf_op jit(solution)/shard_map/ppermute | solution.py:33
  78.4 3.8 %collective-permute-start.7 = (f32[2,1024]{1,0:T(2,128)S(1)}, f32[2,1024]{1,0:T(2,128)S(1)}, u32[]{:S(2)}, u32[]{:S(2)}) collective-permute-start(f32[2,1024]{1,0:T(2,128)S(1)} %broadcast_multiply_fusion), channel_id=1, source_target_pairs={{0,1},{1,2},{2,3},{4,5},{5,6},{6,7},{8,9},{9,10},{10,11},{12,13},{... | collective-permute-start | bytes 24584 | tf_op jit(solution)/shard_map/ppermute | solution.py:33
  82.2 73.1 %collective-permute-start.11 = (bf16[1024,128]{1,0:T(8,128)(2,1)S(1)}, bf16[1024,128]{1,0:T(8,128)(2,1)S(1)}, u32[]{:S(2)}, u32[]{:S(2)}) collective-permute-start(bf16[1024,128]{1,0:T(8,128)(2,1)S(1)} %copy-done.10), channel_id=1, source_target_pairs={{0,12},{8,20},{12,24},{16,4},{20,8},{28,16},{1,13},{9,21},{13,25},... | collective-permute-start | bytes 786440 | tf_op jit(solution)/shard_map/ppermute | solution.py:342
  126.8 28.5 %collective-permute-start.12 = (bf16[1024,128]{1,0:T(8,128)(2,1)S(1)}, bf16[1024,128]{1,0:T(8,128)(2,1)S(1)}, u32[]{:S(2)}, u32[]{:S(2)}) collective-permute-start(bf16[1024,128]{1,0:T(8,128)(2,1)S(1)} %copy-done.10), channel_id=1, source_target_pairs={{4,16},{24,12},{5,17},{25,13},{6,18},{26,14},{7,19},{27,15}} | collective-permute-start | bytes 786440 | tf_op jit(solution)/shard_map/ppermute | solution.py:341
  127.5 27.8 %collective-permute-start.13 = (bf16[1024,128]{1,0:T(8,128)(2,1)S(1)}, bf16[1024,128]{1,0:T(8,128)(2,1)S(1)}, u32[]{:S(2)}, u32[]{:S(2)}) collective-permute-start(bf16[1024,128]{1,0:T(8,128)(2,1)S(1)} %collective-permute-done.10), channel_id=1, source_target_pairs={{8,0},{20,28},{9,1},{21,29},{10,2},{22,30},{11,3},{23,31}} | collective-permute-start | bytes 786440 | tf_op jit(solution)/shard_map/ppermute | solution.py:340
  129.6 21.7 %copy-start.6 = (bf16[1024,256]{1,0:T(8,128)(2,1)S(1)}, bf16[1024,256]{1,0:T(8,128)(2,1)}, u32[]{:S(2)}) copy-start(bf16[1024,256]{1,0:T(8,128)(2,1)} %copy-done.5) | copy-start | bytes 1572868
where the time goes:
time: 158 us
  starting transfers between devices  81.5 us (52%)
  waiting for transfers between devices  34.3 us (22%)
  Pallas kernels  24 us (15%)
  local copies, waits for them, and re-layouts  12.9 us (8%)
  between operations  4.37 us (3%)
    ppermute x1, starting transfers between devices, on_device(): first[3] = lax.ppermute(left[3], 'energy', STRAIGHT)  44.6 us
    ppermute x1, waiting for transfers between devices, on_device(): first[0] = lax.ppermute(left[0], 'energy', STRAIGHT + hops)  17.1 us
    ppermute x1, waiting for transfers between devices, on_device(): first[2] = lax.ppermute(left[2], 'energy', STRAIGHT)  13.9 us
    pallas_call x3, Pallas kernels, photon_of(): pl.pallas_call(functools.partial(photon_body, layout), in_specs=in_specs,...  11.3 us
    unnamed x32, local copies, waits for them, and re-layouts  10.9 us
    pallas_call x5, Pallas kernels, left_of(): pl.pallas_call(functools.partial(left_body, chunk, streamed), in_specs=[p...  9.7 us
    ppermute x1, starting transfers between devices, on_device(): first[1] = lax.ppermute(left[1], 'energy', STRAIGHT)  7.41 us
    ppermute x1, starting transfers between devices, on_device(): second[0] = lax.ppermute(onward, 'energy', EDGES + second_hops)  6.35 us
  transfers between devices with their start and end apart: 17, of which 4 were waited for; matrix products, arithmetic and copies ran while one was open for 2% of the time, Pallas kernels for 13%

commit v1 on v0

--- a/solution.py
+++ b/solution.py
@@ -326,11 +326,12 @@
             correlated += lax.ppermute(sums[n + 1], "energy", route)
 
         middle = left_of(lesser, dipole, MIDDLE)
-        first[0], correlated, *left, middle = lax.optimization_barrier(
-            (first[0], correlated, *left, middle)
+        again = left_of(lesser, dipole, CHUNKS[0])
+        first[0], correlated, *left, middle, again = lax.optimization_barrier(
+            (first[0], correlated, *left, middle, again)
         )
         relays = any_of(own, [by for by, _ in second_hops])
-        onward = either_of(relays, first[0], left[0])
+        onward = either_of(relays, first[0], again)
         second[0] = lax.ppermute(onward, "energy", EDGES + second_hops)
         crossed = lax.ppermute(middle, "energy", CROSS)
         first[2] = lax.ppermute(left[2], "energy", STRAIGHT)

time: 158 us -> 158 us (level)
  Pallas kernels: 24 us -> 26.3 us
    pallas_call x5 -> x6, Pallas kernels: 9.7 us -> 12.1 us  [left_of(): pl.pallas_call(functools.partial(left_body, chunk, streamed), in_specs=[p...]
    unnamed x32 -> x36, local copies, waits for them, and re-layouts: 10.9 us -> 9.66 us
  transfers between devices with their start and end apart: 17 -> 17, of which waited for: 4 -> 4; matrix products, arithmetic and copies ran while one was open for 2% -> 2% of each run, Pallas kernels for 13% -> 15%
where the time goes in v1:
time: 158 us
  starting transfers between devices  81.5 us (52%)
  waiting for transfers between devices  33.1 us (21%)
  Pallas kernels  26.3 us (17%)
  local copies, waits for them, and re-layouts  11.6 us (7%)
  between operations  4.54 us (3%)
    ppermute x1, starting transfers between devices, on_device(): first[3] = lax.ppermute(left[3], 'energy', STRAIGHT)  44.4 us
    ppermute x1, waiting for transfers between devices, on_device(): first[0] = lax.ppermute(left[0], 'energy', STRAIGHT + hops)  15.8 us
    ppermute x1, waiting for transfers between devices, on_device(): first[2] = lax.ppermute(left[2], 'energy', STRAIGHT)  13.9 us
    pallas_call x6, Pallas kernels, left_of(): pl.pallas_call(functools.partial(left_body, chunk, streamed), in_specs=[p...  12.1 us
    pallas_call x3, Pallas kernels, photon_of(): pl.pallas_call(functools.partial(photon_body, layout), in_specs=in_specs,...  11.3 us
    unnamed x36, local copies, waits for them, and re-layouts  9.66 us
    ppermute x1, starting transfers between devices, on_device(): first[1] = lax.ppermute(left[1], 'energy', STRAIGHT)  7.41 us
    ppermute x1, starting transfers between devices, on_device(): second[0] = lax.ppermute(onward, 'energy', EDGES + second_hops)  6.35 us
  transfers between devices with their start and end apart: 17, of which 4 were waited for; matrix products, arithmetic and copies ran while one was open for 2% of the time, Pallas kernels for 15%

profile of v1, /device:TPU:0, one launch (start us, length us, event | category | flops | bytes accessed | tf_op | source)
XLA Modules:
  0.0 157.6 jit_solution(5968825389795485288)
XLA Ops:
  0.6 0.0 copy-start.2
  0.6 0.8 copy-done.13
  1.5 1.0 diagonals.1
  2.5 3.0 %collective-permute-start = (f32[1,2,1024]{2,1,0:T(2,128)S(1)}, f32[1,2,1024]{2,1,0:T(2,128)S(1)}, u32[]{:S(2)}, u32[]{:S(2)}) collective-permute-start(f32[1,2,1024]{2,1,0:T(2,128)S(1)} %diagonals.1), channel_id=1, source_target_pairs={{0,4},{4,0},{8,12},{12,8},{16,20},{20,16},{24,28},{28,24},{1,5},{5... | collective-permute-start | bytes 24584 | tf_op jit(solution)/shard_map/ppermute | solution.py:49
  5.6 4.1 %left.6.refs_0_ = bf16[1024,1024]{1,0:T(8,128)(2,1)S(1)} custom-call(bf16[1,1,2,1024,1024]{4,3,2,1,0:T(8,128)(2,1)} %lesser_ref.13, bf16[1,1024,1024]{2,1,0:T(8,128)(2,1)S(1)} %copy-done.2), custom_call_target="tpu_custom_call" | custom-call | tf_op jit(solution)/shard_map/left/pallas_call | solution.py:148
  9.6 0.0 copy-start.5
  9.6 1.3 copy-done.5
  11.0 0.0 collective-permute-done
  11.0 1.6 collective-permute-start.1
  12.6 0.1 pad_add_fusion
  12.7 0.1 iota_subtract_fusion
  12.7 0.7 collective-permute-start.2
  13.4 0.1 fusion.1
  13.5 0.0 collective-permute-done.2
  13.6 0.7 collective-permute-start.3
  14.2 0.0 copy-start
  14.2 2.2 %copy-done = bf16[1,1,2,1024,1024]{4,3,2,1,0:T(8,128)(2,1)S(1)} copy-done((bf16[1,1,2,1024,1024]{4,3,2,1,0:T(8,128)(2,1)S(1)}, bf16[1,1,2,1024,1024]{4,3,2,1,0:T(8,128)(2,1)}, u32[]{:S(2)}) %copy-start) | copy-done | bytes 4194328
  16.4 0.7 left.7.refs_0_
  17.2 0.8 copy-done.7
  18.0 0.0 collective-permute-done.3
  18.1 0.2 multiply_reduce_fusion
  18.3 0.7 collective-permute-start.4
  18.9 0.7 collective-permute-start.5
  19.6 1.3 collective-permute-start.6
  20.9 0.6 fusion.8
  21.5 2.2 %copy-done.1 = bf16[1,1,2,1024,1024]{4,3,2,1,0:T(8,128)(2,1)S(1)} copy-done((bf16[1,1,2,1024,1024]{4,3,2,1,0:T(8,128)(2,1)S(1)}, bf16[1,1,2,1024,1024]{4,3,2,1,0:T(8,128)(2,1)}, u32[]{:S(2)}) %copy-start.1) | copy-done | bytes 4194328
  23.7 2.4 %left.11.no_ref = bf16[1024,1024]{1,0:T(8,128)(2,1)S(1)} custom-call(bf16[1,1,2,1024,1024]{4,3,2,1,0:T(8,128)(2,1)S(1)} %copy-done.1, bf16[1,1024,1024]{2,1,0:T(8,128)(2,1)S(1)} %copy-done.2), custom_call_target="tpu_custom_call" | custom-call | tf_op jit(solution)/shard_map/left/pallas_call | solution.py:148
  26.1 2.4 %left.10 = bf16[1024,896]{1,0:T(8,128)(2,1)S(1)} custom-call(bf16[1,1,2,1024,1024]{4,3,2,1,0:T(8,128)(2,1)S(1)} %copy-done.1, bf16[1,1024,1024]{2,1,0:T(8,128)(2,1)S(1)} %copy-done.2), custom_call_target="tpu_custom_call" | custom-call | tf_op jit(solution)/shard_map/left/pallas_call | solution.py:148
  28.5 1.8 %left.8.refs_3_ = bf16[1024,640]{1,0:T(8,128)(2,1)S(1)} custom-call(bf16[1,1,2,1024,1024]{4,3,2,1,0:T(8,128)(2,1)S(1)} %copy-done.1, bf16[1,1024,1024]{2,1,0:T(8,128)(2,1)S(1)} %copy-done.2), custom_call_target="tpu_custom_call" | custom-call | tf_op jit(solution)/shard_map/left/pallas_call | solution.py:148
  30.3 0.7 left.9.refs_0_
  31.0 0.7 copy-done.11
  35.0 0.7 stack.37.factors_ref
  35.7 7.4 %collective-permute-start.9 = (bf16[1024,256]{1,0:T(8,128)(2,1)}, bf16[1024,256]{1,0:T(8,128)(2,1)S(1)}, u32[]{:S(2)}, u32[]{:S(2)}) collective-permute-start(bf16[1024,256]{1,0:T(8,128)(2,1)} %copy-done.7), channel_id=1, source_target_pairs={{0,12},{8,20},{12,24},{16,4},{20,8},{28,16},{1,13},{9,21},{13,25},... | collective-permute-start | bytes 1572872 | tf_op jit(solution)/shard_map/ppermute | solution.py:322
  43.1 0.0 collective-permute-done.4
  43.1 0.0 collective-permute-done.5
  43.1 0.0 collective-permute-done.6
  43.2 15.8 %collective-permute-done.1.yes_ref.refs_1_ = bf16[1024,1024]{1,0:T(8,128)(2,1)} collective-permute-done((bf16[1024,1024]{1,0:T(8,128)(2,1)}, bf16[1024,1024]{1,0:T(8,128)(2,1)}, u32[]{:S(2)}, u32[]{:S(2)}) %collective-permute-start.1) | collective-permute-done | bytes 2097184 | tf_op jit(solution)/shard_map/ppermute | solution.py:310
  59.0 1.6 %copy-done.4 = bf16[1024,1024]{1,0:T(8,128)(2,1)S(1)} copy-done((bf16[1024,1024]{1,0:T(8,128)(2,1)S(1)}, bf16[1024,1024]{1,0:T(8,128)(2,1)}, u32[]{:S(2)}) %copy-start.4) | copy-done | bytes 2097176
  60.6 1.9 %either.1 = bf16[1024,1024]{1,0:T(8,128)(2,1)S(1)} custom-call(s32[1]{0:T(128)} %bitcast.18.flag_ref, bf16[1024,1024]{1,0:T(8,128)(2,1)} %collective-permute-done.1.yes_ref.refs_1_, bf16[1024,1024]{1,0:T(8,128)(2,1)S(1)} %copy-done.4), custom_call_target="tpu_custom_call" | custom-call | tf_op jit(solution)/shard_map/either/pallas_call | solution.py:179
  62.5 0.0 copy-start.14
  62.5 6.4 %collective-permute-start.16 = (bf16[1024,1024]{1,0:T(8,128)(2,1)S(1)}, bf16[1024,1024]{1,0:T(8,128)(2,1)S(1)}, u32[]{:S(2)}, u32[]{:S(2)}) collective-permute-start(bf16[1024,1024]{1,0:T(8,128)(2,1)S(1)} %either.1), channel_id=1, source_target_pairs={{12,0},{16,28},{0,16},{28,12},{13,1},{17,29},{1,17},{29,13},{14,2}... | collective-permute-start | bytes 6291464 | tf_op jit(solution)/shard_map/ppermute | solution.py:335
  68.9 1.3 collective-permute-start.14
  70.2 0.7 collective-permute-start.10
  70.9 6.2 %collective-permute-start.15 = (bf16[1024,640]{1,0:T(8,128)(2,1)S(1)}, bf16[1024,640]{1,0:T(8,128)(2,1)S(1)}, u32[]{:S(2)}, u32[]{:S(2)}) collective-permute-start(bf16[1024,640]{1,0:T(8,128)(2,1)S(1)} %left.8.refs_3_), channel_id=1, source_target_pairs={{0,12},{8,20},{12,24},{16,4},{20,8},{28,16},{1,13},{9,21},{13,25},... | collective-permute-start | bytes 3932168 | tf_op jit(solution)/shard_map/ppermute | solution.py:337
  77.1 0.0 copy-start.6
  77.1 0.0 collective-permute-done.9.block_ref
  77.1 1.4 collective-permute-start.8
  78.5 0.0 collective-permute-done.10
  78.5 3.0 %collective-permute-start.7 = (f32[2,1024]{1,0:T(2,128)S(1)}, f32[2,1024]{1,0:T(2,128)S(1)}, u32[]{:S(2)}, u32[]{:S(2)}) collective-permute-start(f32[2,1024]{1,0:T(2,128)S(1)} %broadcast_multiply_fusion), channel_id=1, source_target_pairs={{0,1},{1,2},{2,3},{4,5},{5,6},{6,7},{8,9},{9,10},{10,11},{12,13},{... | collective-permute-start | bytes 24584 | tf_op jit(solution)/shard_map/ppermute | solution.py:33
  81.6 0.8 collective-permute-done.7
  82.4 44.4 %collective-permute-start.11 = (bf16[1024,128]{1,0:T(8,128)(2,1)S(1)}, bf16[1024,128]{1,0:T(8,128)(2,1)S(1)}, u32[]{:S(2)}, u32[]{:S(2)}) collective-permute-start(bf16[1024,128]{1,0:T(8,128)(2,1)S(1)} %copy-done.12), channel_id=1, source_target_pairs={{0,12},{8,20},{12,24},{16,4},{20,8},{28,16},{1,13},{9,21},{13,25},... | collective-permute-start | bytes 786440 | tf_op jit(solution)/shard_map/ppermute | solution.py:343
  126.8 0.0 collective-permute-done.8
  126.8 0.7 collective-permute-start.12
  127.5 0.0 collective-permute-done.16.refs_2_
  127.5 1.5 collective-permute-start.13
  129.0 0.6 slice_bitcast_fusion.3
  129.6 5.2 %photon.3.refs_6_ = bf16[1,1,2,1024,1024]{4,3,2,1,0:T(8,128)(2,1)} custom-call(f32[5]{0:T(128)S(1)} %stack.37.factors_ref, bf16[1,1024,1024]{2,1,0:T(8,128)(2,1)S(1)} %copy-done.2, f32[1,1024]{1,0:T(1,128)S(1)} %get-tuple-element.44.phonon_ref, bf16[1024,1024]{1,0:T(8,128)(2,1)S(1)} %copy-done.6, bf16[1024,1024]{1,0:T(8,128)(2,1)} %collective-permute-done.1.yes_ref.refs_1_, ...), custom_call_target="tpu_custom_call" | custom-call | tf_op jit(solution)/shard_map/photon/pallas_call | solution.py:272
  134.9 13.9 %collective-permute-done.15.refs_4_ = bf16[1024,640]{1,0:T(8,128)(2,1)S(1)} collective-permute-done((bf16[1024,640]{1,0:T(8,128)(2,1)S(1)}, bf16[1024,640]{1,0:T(8,128)(2,1)S(1)}, u32[]{:S(2)}, u32[]{:S(2)}) %collective-permute-start.15) | collective-permute-done | bytes 1310752 | tf_op jit(solution)/shard_map/ppermute | solution.py:337
  148.7 2.6 %collective-permute-done.14.refs_2_.refs_5_ = bf16[1024,896]{1,0:T(8,128)(2,1)S(1)} collective-permute-done((bf16[1024,896]{1,0:T(8,128)(2,1)S(1)}, bf16[1024,896]{1,0:T(8,128)(2,1)S(1)}, u32[]{:S(2)}, u32[]{:S(2)}) %collective-permute-start.14) | collective-permute-done | bytes 1835040 | tf_op jit(solution)/shard_map/ppermute | solution.py:336
  151.3 4.0 %photon.4.refs_4_ = bf16[1,1,2,1024,1024]{4,3,2,1,0:T(8,128)(2,1)} custom-call(f32[5]{0:T(128)S(1)} %stack.37.factors_ref, bf16[1,1024,1024]{2,1,0:T(8,128)(2,1)S(1)} %copy-done.2, f32[1,1024]{1,0:T(1,128)S(1)} %get-tuple-element.44.phonon_ref, bf16[1024,256]{1,0:T(8,128)(2,1)S(1)} %copy-done.8, ...), custom_call_target="tpu_custom_call", output_to_operand_aliasing={{}: (9, {})} | custom-call | tf_op jit(solution)/shard_map/photon/pallas_call | solution.py:272
  155.3 0.0 collective-permute-done.11.refs_1_
  155.3 0.0 collective-permute-done.12.refs_2_
  155.3 0.0 collective-permute-done.13.refs_3_
  155.3 2.1 %photon.5 = bf16[1,1,2,1024,1024]{4,3,2,1,0:T(8,128)(2,1)} custom-call(f32[5]{0:T(128)S(1)} %stack.37.factors_ref, bf16[1,1024,1024]{2,1,0:T(8,128)(2,1)S(1)} %copy-done.2, f32[1,1024]{1,0:T(1,128)S(1)} %get-tuple-element.44.phonon_ref, bf16[1024,128]{1,0:T(8,128)(2,1)S(1)} %copy-done.12, ...), custom_call_target="tpu_custom_call", output_to_operand_aliasing={{}: (7, {})} | custom-call | tf_op jit(solution)/shard_map/photon/pallas_call | solution.py:272
  (41 shorter events, 0.3 us)
Async XLA Ops:
  0.6 4.9 %copy-start.2 = (bf16[1,1024,1024]{2,1,0:T(8,128)(2,1)S(1)}, bf16[1,1024,1024]{2,1,0:T(8,128)(2,1)}, u32[]{:S(2)}) copy-start(bf16[1,1024,1024]{2,1,0:T(8,128)(2,1)} %dipole_ref.17) | copy-start | bytes 6291460
  0.6 0.8 copy-start.13
  2.5 8.4 %collective-permute-start = (f32[1,2,1024]{2,1,0:T(2,128)S(1)}, f32[1,2,1024]{2,1,0:T(2,128)S(1)}, u32[]{:S(2)}, u32[]{:S(2)}) collective-permute-start(f32[1,2,1024]{2,1,0:T(2,128)S(1)} %diagonals.1), channel_id=1, source_target_pairs={{0,4},{4,0},{8,12},{12,8},{16,20},{20,16},{24,28},{28,24},{1,5},{5... | collective-permute-start | bytes 24584 | tf_op jit(solution)/shard_map/ppermute | solution.py:49
  5.6 5.4 %copy-start.17 = (s32[6]{0:T(128)S(1)}, s32[6]{0:T(128)}, u32[]{:S(2)}) copy-start(s32[6]{0:T(128)} %param.13) | copy-start | bytes 76
  5.6 7.1 %copy-start.16 = (f32[2,6]{1,0:T(2,128)S(1)}, f32[2,6]{1,0:T(2,128)}, u32[]{:S(2)}) copy-start(f32[2,6]{1,0:T(2,128)} %param.14) | copy-start | bytes 148
  9.6 1.3 copy-start.5
  11.0 48.0 %collective-permute-start.1 = (bf16[1024,1024]{1,0:T(8,128)(2,1)}, bf16[1024,1024]{1,0:T(8,128)(2,1)}, u32[]{:S(2)}, u32[]{:S(2)}) collective-permute-start(bf16[1024,1024]{1,0:T(8,128)(2,1)} %copy-done.5), channel_id=1, source_target_pairs={{0,12},{8,20},{12,24},{16,4},{20,8},{28,16},{4,0},{24,28},{1,13},{... | collective-permute-start | bytes 6291464 | tf_op jit(solution)/shard_map/ppermute | solution.py:310
  12.7 0.8 collective-permute-start.2
  13.6 4.4 %collective-permute-start.3 = (f32[4,2,1024]{2,1,0:T(2,128)S(1)}, f32[4,2,1024]{2,1,0:T(2,128)S(1)}, u32[]{:S(2)}, u32[]{:S(2)}) collective-permute-start(f32[4,2,1024]{2,1,0:T(2,128)S(1)} %pad_maximum_fusion.1), channel_id=1, source_target_pairs={{4,24},{24,4},{5,25},{25,5},{6,26},{26,6},{7,27},{27,7}} | collective-permute-start | bytes 98312 | tf_op jit(solution)/shard_map/ppermute | solution.py:314
  14.2 2.2 %copy-start = (bf16[1,1,2,1024,1024]{4,3,2,1,0:T(8,128)(2,1)S(1)}, bf16[1,1,2,1024,1024]{4,3,2,1,0:T(8,128)(2,1)}, u32[]{:S(2)}) copy-start(bf16[1,1,2,1024,1024]{4,3,2,1,0:T(8,128)(2,1)} %lesser_ref.13) | copy-start | bytes 12582916
  16.4 4.5 %copy-start.15 = (f32[1,3]{1,0:T(1,128)S(1)}, f32[1,3]{1,0:T(1,128)}, u32[]{:S(2)}) copy-start(f32[1,3]{1,0:T(1,128)} %param.11) | copy-start | bytes 40
  17.2 0.8 copy-start.7
  18.3 24.8 %collective-permute-start.4 = (f32[2,1024]{1,0:T(2,128)S(1)}, f32[2,1024]{1,0:T(2,128)S(1)}, u32[]{:S(2)}, u32[]{:S(2)}) collective-permute-start(f32[2,1024]{1,0:T(2,128)S(1)} %get-tuple-element.36), channel_id=1, source_target_pairs={{4,12},{24,16},{5,13},{25,17},{6,14},{26,18},{7,15},{27,19}} | collective-permute-start | bytes 24584 | tf_op jit(solution)/shard_map/ppermute | solution.py:326
  18.9 24.2 %collective-permute-start.5 = (f32[2,1024]{1,0:T(2,128)S(1)}, f32[2,1024]{1,0:T(2,128)S(1)}, u32[]{:S(2)}, u32[]{:S(2)}) collective-permute-start(f32[2,1024]{1,0:T(2,128)S(1)} %get-tuple-element.38), channel_id=1, source_target_pairs={{4,20},{24,8},{5,21},{25,9},{6,22},{26,10},{7,23},{27,11}} | collective-permute-start | bytes 24584 | tf_op jit(solution)/shard_map/ppermute | solution.py:326
  19.6 23.5 %collective-permute-start.6 = (f32[2,1024]{1,0:T(2,128)S(1)}, f32[2,1024]{1,0:T(2,128)S(1)}, u32[]{:S(2)}, u32[]{:S(2)}) collective-permute-start(f32[2,1024]{1,0:T(2,128)S(1)} %get-tuple-element.37), channel_id=1, source_target_pairs={{4,28},{24,0},{5,29},{25,1},{6,30},{26,2},{7,31},{27,3}} | collective-permute-start | bytes 24584 | tf_op jit(solution)/shard_map/ppermute | solution.py:326
  21.5 2.2 %copy-start.1 = (bf16[1,1,2,1024,1024]{4,3,2,1,0:T(8,128)(2,1)S(1)}, bf16[1,1,2,1024,1024]{4,3,2,1,0:T(8,128)(2,1)}, u32[]{:S(2)}) copy-start(bf16[1,1,2,1024,1024]{4,3,2,1,0:T(8,128)(2,1)} %lesser_ref.13) | copy-start | bytes 12582916
  26.1 2.4 %copy-start.3 = (bf16[1024,1024]{1,0:T(8,128)(2,1)}, bf16[1024,1024]{1,0:T(8,128)(2,1)S(1)}, u32[]{:S(2)}) copy-start(bf16[1024,1024]{1,0:T(8,128)(2,1)S(1)} %left.11.no_ref) | copy-start | bytes 6291460
  28.5 1.8 %copy-start.9 = (bf16[1024,896]{1,0:T(8,128)(2,1)}, bf16[1024,896]{1,0:T(8,128)(2,1)S(1)}, u32[]{:S(2)}) copy-start(bf16[1024,896]{1,0:T(8,128)(2,1)S(1)} %left.10) | copy-start | bytes 5505028
  31.0 0.7 copy-start.11
  35.7 41.4 %collective-permute-start.9 = (bf16[1024,256]{1,0:T(8,128)(2,1)}, bf16[1024,256]{1,0:T(8,128)(2,1)S(1)}, u32[]{:S(2)}, u32[]{:S(2)}) collective-permute-start(bf16[1024,256]{1,0:T(8,128)(2,1)} %copy-done.7), channel_id=1, source_target_pairs={{0,12},{8,20},{12,24},{16,4},{20,8},{28,16},{1,13},{9,21},{13,25},... | collective-permute-start | bytes 1572872 | tf_op jit(solution)/shard_map/ppermute | solution.py:322
  59.0 1.6 %copy-start.4 = (bf16[1024,1024]{1,0:T(8,128)(2,1)S(1)}, bf16[1024,1024]{1,0:T(8,128)(2,1)}, u32[]{:S(2)}) copy-start(bf16[1024,1024]{1,0:T(8,128)(2,1)} %copy-done.3) | copy-start | bytes 6291460
  60.6 8.3 %copy-start.10 = (bf16[1024,896]{1,0:T(8,128)(2,1)S(1)}, bf16[1024,896]{1,0:T(8,128)(2,1)}, u32[]{:S(2)}) copy-start(bf16[1024,896]{1,0:T(8,128)(2,1)} %copy-done.9) | copy-start | bytes 5505028
  60.6 9.6 %copy-start.12 = (bf16[1024,128]{1,0:T(8,128)(2,1)S(1)}, bf16[1024,128]{1,0:T(8,128)(2,1)}, u32[]{:S(2)}) copy-start(bf16[1024,128]{1,0:T(8,128)(2,1)} %copy-done.11) | copy-start | bytes 786436
  62.5 14.6 %copy-start.14 = (f32[1,1024]{1,0:T(1,128)S(1)}, f32[1,1024]{1,0:T(1,128)}, u32[]{:S(2)}) copy-start(f32[1,1024]{1,0:T(1,128)} %param.15) | copy-start | bytes 12292
  62.5 65.0 %collective-permute-start.16 = (bf16[1024,1024]{1,0:T(8,128)(2,1)S(1)}, bf16[1024,1024]{1,0:T(8,128)(2,1)S(1)}, u32[]{:S(2)}, u32[]{:S(2)}) collective-permute-start(bf16[1024,1024]{1,0:T(8,128)(2,1)S(1)} %either.1), channel_id=1, source_target_pairs={{12,0},{16,28},{0,16},{28,12},{13,1},{17,29},{1,17},{29,13},{14,2}... | collective-permute-start | bytes 6291464 | tf_op jit(solution)/shard_map/ppermute | solution.py:335
  68.9 82.4 %collective-permute-start.14 = (bf16[1024,896]{1,0:T(8,128)(2,1)S(1)}, bf16[1024,896]{1,0:T(8,128)(2,1)S(1)}, u32[]{:S(2)}, u32[]{:S(2)}) collective-permute-start(bf16[1024,896]{1,0:T(8,128)(2,1)S(1)} %copy-done.10), channel_id=1, source_target_pairs={{4,16},{12,0},{16,28},{24,12},{5,17},{13,1},{17,29},{25,13},{6,18}... | collective-permute-start | bytes 5505032 | tf_op jit(solution)/shard_map/ppermute | solution.py:336
  70.2 8.3 %collective-permute-start.10 = (bf16[1024,128]{1,0:T(8,128)(2,1)S(1)}, bf16[1024,128]{1,0:T(8,128)(2,1)S(1)}, u32[]{:S(2)}, u32[]{:S(2)}) collective-permute-start(bf16[1024,128]{1,0:T(8,128)(2,1)S(1)} %copy-done.12), channel_id=1, source_target_pairs={{12,8},{16,20},{13,9},{17,21},{14,10},{18,22},{15,11},{19,23}} | collective-permute-start | bytes 786440 | tf_op jit(solution)/shard_map/ppermute | solution.py:338
  70.9 77.9 %collective-permute-start.15 = (bf16[1024,640]{1,0:T(8,128)(2,1)S(1)}, bf16[1024,640]{1,0:T(8,128)(2,1)S(1)}, u32[]{:S(2)}, u32[]{:S(2)}) collective-permute-start(bf16[1024,640]{1,0:T(8,128)(2,1)S(1)} %left.8.refs_3_), channel_id=1, source_target_pairs={{0,12},{8,20},{12,24},{16,4},{20,8},{28,16},{1,13},{9,21},{13,25},... | collective-permute-start | bytes 3932168 | tf_op jit(solution)/shard_map/ppermute | solution.py:337
  77.1 52.6 %copy-start.6 = (bf16[1024,1024]{1,0:T(8,128)(2,1)S(1)}, bf16[1024,1024]{1,0:T(8,128)(2,1)}, u32[]{:S(2)}) copy-start(bf16[1024,1024]{1,0:T(8,128)(2,1)} %copy-done.5) | copy-start | bytes 6291460
  77.1 49.7 %collective-permute-start.8 = (f32[2,1024]{1,0:T(2,128)S(1)}, f32[2,1024]{1,0:T(2,128)S(1)}, u32[]{:S(2)}, u32[]{:S(2)}) collective-permute-start(f32[2,1024]{1,0:T(2,128)S(1)} %held.2), channel_id=1, source_target_pairs={{1,0},{2,1},{3,2},{5,4},{6,5},{7,6},{9,8},{10,9},{11,10},{13,12},{... | collective-permute-start | bytes 24584 | tf_op jit(solution)/shard_map/ppermute | solution.py:33
  78.5 3.8 %collective-permute-start.7 = (f32[2,1024]{1,0:T(2,128)S(1)}, f32[2,1024]{1,0:T(2,128)S(1)}, u32[]{:S(2)}, u32[]{:S(2)}) collective-permute-start(f32[2,1024]{1,0:T(2,128)S(1)} %broadcast_multiply_fusion), channel_id=1, source_target_pairs={{0,1},{1,2},{2,3},{4,5},{5,6},{6,7},{8,9},{9,10},{10,11},{12,13},{... | collective-permute-start | bytes 24584 | tf_op jit(solution)/shard_map/ppermute | solution.py:33
  82.4 72.9 %collective-permute-start.11 = (bf16[1024,128]{1,0:T(8,128)(2,1)S(1)}, bf16[1024,128]{1,0:T(8,128)(2,1)S(1)}, u32[]{:S(2)}, u32[]{:S(2)}) collective-permute-start(bf16[1024,128]{1,0:T(8,128)(2,1)S(1)} %copy-done.12), channel_id=1, source_target_pairs={{0,12},{8,20},{12,24},{16,4},{20,8},{28,16},{1,13},{9,21},{13,25},... | collective-permute-start | bytes 786440 | tf_op jit(solution)/shard_map/ppermute | solution.py:343
  126.8 28.5 %collective-permute-start.12 = (bf16[1024,128]{1,0:T(8,128)(2,1)S(1)}, bf16[1024,128]{1,0:T(8,128)(2,1)S(1)}, u32[]{:S(2)}, u32[]{:S(2)}) collective-permute-start(bf16[1024,128]{1,0:T(8,128)(2,1)S(1)} %copy-done.12), channel_id=1, source_target_pairs={{4,16},{24,12},{5,17},{25,13},{6,18},{26,14},{7,19},{27,15}} | collective-permute-start | bytes 786440 | tf_op jit(solution)/shard_map/ppermute | solution.py:342
  127.5 27.8 %collective-permute-start.13 = (bf16[1024,128]{1,0:T(8,128)(2,1)S(1)}, bf16[1024,128]{1,0:T(8,128)(2,1)S(1)}, u32[]{:S(2)}, u32[]{:S(2)}) collective-permute-start(bf16[1024,128]{1,0:T(8,128)(2,1)S(1)} %collective-permute-done.10), channel_id=1, source_target_pairs={{8,0},{20,28},{9,1},{21,29},{10,2},{22,30},{11,3},{23,31}} | collective-permute-start | bytes 786440 | tf_op jit(solution)/shard_map/ppermute | solution.py:341
  129.6 21.7 %copy-start.8 = (bf16[1024,256]{1,0:T(8,128)(2,1)S(1)}, bf16[1024,256]{1,0:T(8,128)(2,1)}, u32[]{:S(2)}) copy-start(bf16[1024,256]{1,0:T(8,128)(2,1)} %copy-done.7) | copy-start | bytes 1572868

commit v2 on v0

--- a/solution.py
+++ b/solution.py
@@ -161,15 +161,11 @@
     )(lesser, dipole)
 
 
-def either_body(flag_ref, yes_ref, no_ref, out_ref):
-    height = out_ref.shape[0]
-    rows = height // 16
-
+def either_body(flag_ref, yes_ref, no_ref, out_ref, arrived):
     def copied_from(ref):
-        @pl.loop(0, height // rows)
-        def _(i):
-            at = pl.ds(pl.multiple_of(i * rows, rows), rows)
-            out_ref[at] = ref[at]
+        copy = pltpu.make_async_copy(ref, out_ref, arrived)
+        copy.start()
+        copy.wait()
 
     pl.when(flag_ref[0] != 0)(lambda: copied_from(yes_ref))
     pl.when(flag_ref[0] == 0)(lambda: copied_from(no_ref))
@@ -180,11 +176,12 @@
         either_body,
         in_specs=[
             pl.BlockSpec(memory_space=pltpu.SMEM),
-            pl.BlockSpec(memory_space=pltpu.VMEM),
-            pl.BlockSpec(memory_space=pltpu.VMEM),
+            pl.BlockSpec(memory_space=pl.ANY),
+            pl.BlockSpec(memory_space=pl.ANY),
         ],
         out_specs=pl.BlockSpec(memory_space=pltpu.VMEM),
         out_shape=jax.ShapeDtypeStruct(yes.shape, yes.dtype),
+        scratch_shapes=[pltpu.SemaphoreType.DMA],
         compiler_params=pltpu.CompilerParams(vmem_limit_bytes=VMEM_BYTES),
         name="either",
     )(flag.astype(jnp.int32).reshape(1), yes, no)

time: 158 us -> 157 us (level)
  starting transfers between devices: 81.5 us -> 76 us
  waiting for transfers between devices: 34.3 us -> 38.8 us
    ppermute x1, waiting for transfers between devices: 13.9 us -> 19.5 us  [on_device(): first[2] = lax.ppermute(left[2], 'energy', STRAIGHT)]
    ppermute x1, starting transfers between devices: 44.6 us -> 40.6 us  [on_device(): first[3] = lax.ppermute(left[3], 'energy', STRAIGHT)]
where the time goes in v2:
time: 157 us; the launch traced here: 156 us
  starting transfers between devices  76 us (48%)
  waiting for transfers between devices  38.8 us (25%)
  Pallas kernels  23.8 us (15%)
  local copies, waits for them, and re-layouts  12.9 us (8%)
  between operations  4.37 us (3%)
    ppermute x1, starting transfers between devices, on_device(): first[3] = lax.ppermute(left[3], 'energy', STRAIGHT)  40.6 us
    ppermute x1, waiting for transfers between devices, on_device(): first[2] = lax.ppermute(left[2], 'energy', STRAIGHT)  19.5 us
    ppermute x1, waiting for transfers between devices, on_device(): first[0] = lax.ppermute(left[0], 'energy', STRAIGHT + hops)  17.1 us
    pallas_call x3, Pallas kernels, photon_of(): pl.pallas_call(functools.partial(photon_body, layout), in_specs=in_specs,...  11.3 us
    unnamed x32, local copies, waits for them, and re-layouts  10.9 us
    pallas_call x5, Pallas kernels, left_of(): pl.pallas_call(functools.partial(left_body, chunk, streamed), in_specs=[p...  9.7 us
    ppermute x1, starting transfers between devices, on_device(): first[1] = lax.ppermute(left[1], 'energy', STRAIGHT)  7.41 us
    ppermute x1, starting transfers between devices, on_device(): first[2] = lax.ppermute(left[2], 'energy', STRAIGHT)  6.16 us
  transfers between devices with their start and end apart: 17, of which 4 were waited for; matrix products, arithmetic and copies ran while one was open for 2% of the time, Pallas kernels for 13%

profile of v2, /device:TPU:0, one launch (start us, length us, event | category | flops | bytes accessed | tf_op | source)
XLA Modules:
  0.0 156.4 jit_solution(10618838735155908149)
XLA Ops:
  0.6 0.8 copy-done.11
  1.5 1.0 diagonals.1
  2.5 3.0 %collective-permute-start = (f32[1,2,1024]{2,1,0:T(2,128)S(1)}, f32[1,2,1024]{2,1,0:T(2,128)S(1)}, u32[]{:S(2)}, u32[]{:S(2)}) collective-permute-start(f32[1,2,1024]{2,1,0:T(2,128)S(1)} %diagonals.1), channel_id=1, source_target_pairs={{0,4},{4,0},{8,12},{12,8},{16,20},{20,16},{24,28},{28,24},{1,5},{5... | collective-permute-start | bytes 24584 | tf_op jit(solution)/shard_map/ppermute | solution.py:49
  5.6 4.1 %left.5.no_ref.refs_0_ = bf16[1024,1024]{1,0:T(8,128)(2,1)S(1)} custom-call(bf16[1,1,2,1024,1024]{4,3,2,1,0:T(8,128)(2,1)} %lesser_ref.11, bf16[1,1024,1024]{2,1,0:T(8,128)(2,1)S(1)} %copy-done.2), custom_call_target="tpu_custom_call" | custom-call | tf_op jit(solution)/shard_map/left/pallas_call | solution.py:148
  9.6 0.0 copy-start.3
  9.6 1.3 copy-done.3
  11.0 0.0 collective-permute-done
  11.0 1.6 %collective-permute-start.1 = (bf16[1024,1024]{1,0:T(8,128)(2,1)}, bf16[1024,1024]{1,0:T(8,128)(2,1)}, u32[]{:S(2)}, u32[]{:S(2)}) collective-permute-start(bf16[1024,1024]{1,0:T(8,128)(2,1)} %copy-done.3), channel_id=1, source_target_pairs={{0,12},{8,20},{12,24},{16,4},{20,8},{28,16},{4,0},{24,28},{1,13},{... | collective-permute-start | bytes 6291464 | tf_op jit(solution)/shard_map/ppermute | solution.py:307
  12.6 0.1 pad_add_fusion
  12.7 0.1 iota_subtract_fusion
  12.7 0.7 collective-permute-start.2
  13.4 0.1 fusion.1
  13.5 0.0 collective-permute-done.2
  13.6 0.7 collective-permute-start.3
  14.2 0.0 copy-start
  14.2 2.2 %copy-done = bf16[1,1,2,1024,1024]{4,3,2,1,0:T(8,128)(2,1)S(1)} copy-done((bf16[1,1,2,1024,1024]{4,3,2,1,0:T(8,128)(2,1)S(1)}, bf16[1,1,2,1024,1024]{4,3,2,1,0:T(8,128)(2,1)}, u32[]{:S(2)}) %copy-start) | copy-done | bytes 4194328
  16.4 0.7 left.6.refs_0_
  17.2 0.0 copy-start.5
  17.2 0.8 copy-done.5
  18.0 0.0 collective-permute-done.3
  18.1 0.2 multiply_reduce_fusion
  18.3 0.7 collective-permute-start.4
  18.9 0.7 collective-permute-start.5
  19.6 1.3 collective-permute-start.6
  20.9 0.6 fusion.8
  21.5 2.2 %copy-done.1 = bf16[1,1,2,1024,1024]{4,3,2,1,0:T(8,128)(2,1)S(1)} copy-done((bf16[1,1,2,1024,1024]{4,3,2,1,0:T(8,128)(2,1)S(1)}, bf16[1,1,2,1024,1024]{4,3,2,1,0:T(8,128)(2,1)}, u32[]{:S(2)}) %copy-start.1) | copy-done | bytes 4194328
  23.7 2.4 %left.9 = bf16[1024,896]{1,0:T(8,128)(2,1)S(1)} custom-call(bf16[1,1,2,1024,1024]{4,3,2,1,0:T(8,128)(2,1)S(1)} %copy-done.1, bf16[1,1024,1024]{2,1,0:T(8,128)(2,1)S(1)} %copy-done.2), custom_call_target="tpu_custom_call" | custom-call | tf_op jit(solution)/shard_map/left/pallas_call | solution.py:148
  26.1 0.0 copy-start.7
  26.1 1.2 copy-done.7
  27.3 1.8 %left.7.refs_3_ = bf16[1024,640]{1,0:T(8,128)(2,1)S(1)} custom-call(bf16[1,1,2,1024,1024]{4,3,2,1,0:T(8,128)(2,1)S(1)} %copy-done.1, bf16[1,1024,1024]{2,1,0:T(8,128)(2,1)S(1)} %copy-done.2), custom_call_target="tpu_custom_call" | custom-call | tf_op jit(solution)/shard_map/left/pallas_call | solution.py:148
  29.2 0.7 left.8.refs_0_
  29.9 0.7 copy-done.9
  33.6 0.8 stack.37.factors_ref
  34.4 7.4 %collective-permute-start.9 = (bf16[1024,256]{1,0:T(8,128)(2,1)}, bf16[1024,256]{1,0:T(8,128)(2,1)S(1)}, u32[]{:S(2)}, u32[]{:S(2)}) collective-permute-start(bf16[1024,256]{1,0:T(8,128)(2,1)} %copy-done.5), channel_id=1, source_target_pairs={{0,12},{8,20},{12,24},{16,4},{20,8},{28,16},{1,13},{9,21},{13,25},... | collective-permute-start | bytes 1572872 | tf_op jit(solution)/shard_map/ppermute | solution.py:319
  41.8 0.0 collective-permute-done.4
  41.9 0.0 collective-permute-done.5
  41.9 0.0 collective-permute-done.6
  41.9 17.1 %collective-permute-done.1.yes_ref.refs_1_ = bf16[1024,1024]{1,0:T(8,128)(2,1)} collective-permute-done((bf16[1024,1024]{1,0:T(8,128)(2,1)}, bf16[1024,1024]{1,0:T(8,128)(2,1)}, u32[]{:S(2)}, u32[]{:S(2)}) %collective-permute-start.1) | collective-permute-done | bytes 2097184 | tf_op jit(solution)/shard_map/ppermute | solution.py:307
  59.0 1.6 %copy-done.4 = bf16[1024,1024]{1,0:T(8,128)(2,1)S(1)} copy-done((bf16[1024,1024]{1,0:T(8,128)(2,1)S(1)}, bf16[1024,1024]{1,0:T(8,128)(2,1)}, u32[]{:S(2)}) %copy-start.4) | copy-done | bytes 2097176
  60.6 1.7 %either.1 = bf16[1024,1024]{1,0:T(8,128)(2,1)S(1)} custom-call(s32[1]{0:T(128)} %bitcast.18.flag_ref, bf16[1024,1024]{1,0:T(8,128)(2,1)} %collective-permute-done.1.yes_ref.refs_1_, bf16[1024,1024]{1,0:T(8,128)(2,1)S(1)} %copy-done.4), custom_call_target="tpu_custom_call" | custom-call | tf_op jit(solution)/shard_map/either/pallas_call | solution.py:175
  62.3 0.0 copy-start.12
  62.3 4.9 %collective-permute-start.16 = (bf16[1024,1024]{1,0:T(8,128)(2,1)S(1)}, bf16[1024,1024]{1,0:T(8,128)(2,1)S(1)}, u32[]{:S(2)}, u32[]{:S(2)}) collective-permute-start(bf16[1024,1024]{1,0:T(8,128)(2,1)S(1)} %either.1), channel_id=1, source_target_pairs={{12,0},{16,28},{0,16},{28,12},{13,1},{17,29},{1,17},{29,13},{14,2}... | collective-permute-start | bytes 6291464 | tf_op jit(solution)/shard_map/ppermute | solution.py:331
  67.2 1.3 collective-permute-start.14
  68.6 0.7 collective-permute-start.10
  69.2 6.2 %collective-permute-start.15 = (bf16[1024,640]{1,0:T(8,128)(2,1)S(1)}, bf16[1024,640]{1,0:T(8,128)(2,1)S(1)}, u32[]{:S(2)}, u32[]{:S(2)}) collective-permute-start(bf16[1024,640]{1,0:T(8,128)(2,1)S(1)} %left.7.refs_3_), channel_id=1, source_target_pairs={{0,12},{8,20},{12,24},{16,4},{20,8},{28,16},{1,13},{9,21},{13,25},... | collective-permute-start | bytes 3932168 | tf_op jit(solution)/shard_map/ppermute | solution.py:333
  75.4 0.0 collective-permute-done.9.block_ref
  75.5 1.3 collective-permute-start.8
  76.8 0.0 collective-permute-done.10
  76.8 3.0 %collective-permute-start.7 = (f32[2,1024]{1,0:T(2,128)S(1)}, f32[2,1024]{1,0:T(2,128)S(1)}, u32[]{:S(2)}, u32[]{:S(2)}) collective-permute-start(f32[2,1024]{1,0:T(2,128)S(1)} %broadcast_multiply_fusion), channel_id=1, source_target_pairs={{0,1},{1,2},{2,3},{4,5},{5,6},{6,7},{8,9},{9,10},{10,11},{12,13},{... | collective-permute-start | bytes 24584 | tf_op jit(solution)/shard_map/ppermute | solution.py:33
  79.8 0.8 collective-permute-done.7
  80.6 40.6 %collective-permute-start.11 = (bf16[1024,128]{1,0:T(8,128)(2,1)S(1)}, bf16[1024,128]{1,0:T(8,128)(2,1)S(1)}, u32[]{:S(2)}, u32[]{:S(2)}) collective-permute-start(bf16[1024,128]{1,0:T(8,128)(2,1)S(1)} %copy-done.10), channel_id=1, source_target_pairs={{0,12},{8,20},{12,24},{16,4},{20,8},{28,16},{1,13},{9,21},{13,25},... | collective-permute-start | bytes 786440 | tf_op jit(solution)/shard_map/ppermute | solution.py:339
  121.2 0.0 collective-permute-done.8
  121.2 0.7 collective-permute-start.12
  121.9 0.0 collective-permute-done.16.refs_2_
  121.9 1.5 collective-permute-start.13
  123.4 0.6 slice_bitcast_fusion.3
  124.0 5.2 %photon.3.refs_6_ = bf16[1,1,2,1024,1024]{4,3,2,1,0:T(8,128)(2,1)} custom-call(f32[5]{0:T(128)S(1)} %stack.37.factors_ref, bf16[1,1024,1024]{2,1,0:T(8,128)(2,1)S(1)} %copy-done.2, f32[1,1024]{1,0:T(1,128)S(1)} %get-tuple-element.42.phonon_ref, bf16[1024,1024]{1,0:T(8,128)(2,1)S(1)} %copy-done.4, bf16[1024,1024]{1,0:T(8,128)(2,1)} %collective-permute-done.1.yes_ref.refs_1_, ...), custom_call_target="tpu_custom_call" | custom-call | tf_op jit(solution)/shard_map/photon/pallas_call | solution.py:269
  129.2 19.5 %collective-permute-done.15.refs_4_ = bf16[1024,640]{1,0:T(8,128)(2,1)S(1)} collective-permute-done((bf16[1024,640]{1,0:T(8,128)(2,1)S(1)}, bf16[1024,640]{1,0:T(8,128)(2,1)S(1)}, u32[]{:S(2)}, u32[]{:S(2)}) %collective-permute-start.15) | collective-permute-done | bytes 1310752 | tf_op jit(solution)/shard_map/ppermute | solution.py:333
  148.7 1.4 collective-permute-done.14.refs_2_.refs_5_
  150.1 4.0 %photon.4.refs_4_ = bf16[1,1,2,1024,1024]{4,3,2,1,0:T(8,128)(2,1)} custom-call(f32[5]{0:T(128)S(1)} %stack.37.factors_ref, bf16[1,1024,1024]{2,1,0:T(8,128)(2,1)S(1)} %copy-done.2, f32[1,1024]{1,0:T(1,128)S(1)} %get-tuple-element.42.phonon_ref, bf16[1024,256]{1,0:T(8,128)(2,1)S(1)} %copy-done.6, ...), custom_call_target="tpu_custom_call", output_to_operand_aliasing={{}: (9, {})} | custom-call | tf_op jit(solution)/shard_map/photon/pallas_call | solution.py:269
  154.2 0.0 collective-permute-done.11.refs_1_
  154.2 0.0 collective-permute-done.12.refs_2_
  154.2 0.0 collective-permute-done.13.refs_3_
  154.2 2.1 %photon.5 = bf16[1,1,2,1024,1024]{4,3,2,1,0:T(8,128)(2,1)} custom-call(f32[5]{0:T(128)S(1)} %stack.37.factors_ref, bf16[1,1024,1024]{2,1,0:T(8,128)(2,1)S(1)} %copy-done.2, f32[1,1024]{1,0:T(1,128)S(1)} %get-tuple-element.42.phonon_ref, bf16[1024,128]{1,0:T(8,128)(2,1)S(1)} %copy-done.10, ...), custom_call_target="tpu_custom_call", output_to_operand_aliasing={{}: (7, {})} | custom-call | tf_op jit(solution)/shard_map/photon/pallas_call | solution.py:269
  (36 shorter events, 0.3 us)
Async XLA Ops:
  0.6 4.9 %copy-start.2 = (bf16[1,1024,1024]{2,1,0:T(8,128)(2,1)S(1)}, bf16[1,1024,1024]{2,1,0:T(8,128)(2,1)}, u32[]{:S(2)}) copy-start(bf16[1,1024,1024]{2,1,0:T(8,128)(2,1)} %dipole_ref.15) | copy-start | bytes 6291460
  0.6 0.8 copy-start.11
  2.5 8.4 %collective-permute-start = (f32[1,2,1024]{2,1,0:T(2,128)S(1)}, f32[1,2,1024]{2,1,0:T(2,128)S(1)}, u32[]{:S(2)}, u32[]{:S(2)}) collective-permute-start(f32[1,2,1024]{2,1,0:T(2,128)S(1)} %diagonals.1), channel_id=1, source_target_pairs={{0,4},{4,0},{8,12},{12,8},{16,20},{20,16},{24,28},{28,24},{1,5},{5... | collective-permute-start | bytes 24584 | tf_op jit(solution)/shard_map/ppermute | solution.py:49
  5.6 5.4 %copy-start.15 = (s32[6]{0:T(128)S(1)}, s32[6]{0:T(128)}, u32[]{:S(2)}) copy-start(s32[6]{0:T(128)} %param.13) | copy-start | bytes 76
  5.6 7.1 %copy-start.14 = (f32[2,6]{1,0:T(2,128)S(1)}, f32[2,6]{1,0:T(2,128)}, u32[]{:S(2)}) copy-start(f32[2,6]{1,0:T(2,128)} %param.14) | copy-start | bytes 148
  9.6 1.3 copy-start.3
  11.0 48.0 %collective-permute-start.1 = (bf16[1024,1024]{1,0:T(8,128)(2,1)}, bf16[1024,1024]{1,0:T(8,128)(2,1)}, u32[]{:S(2)}, u32[]{:S(2)}) collective-permute-start(bf16[1024,1024]{1,0:T(8,128)(2,1)} %copy-done.3), channel_id=1, source_target_pairs={{0,12},{8,20},{12,24},{16,4},{20,8},{28,16},{4,0},{24,28},{1,13},{... | collective-permute-start | bytes 6291464 | tf_op jit(solution)/shard_map/ppermute | solution.py:307
  12.7 0.8 collective-permute-start.2
  13.6 4.4 %collective-permute-start.3 = (f32[4,2,1024]{2,1,0:T(2,128)S(1)}, f32[4,2,1024]{2,1,0:T(2,128)S(1)}, u32[]{:S(2)}, u32[]{:S(2)}) collective-permute-start(f32[4,2,1024]{2,1,0:T(2,128)S(1)} %pad_maximum_fusion.1), channel_id=1, source_target_pairs={{4,24},{24,4},{5,25},{25,5},{6,26},{26,6},{7,27},{27,7}} | collective-permute-start | bytes 98312 | tf_op jit(solution)/shard_map/ppermute | solution.py:311
  14.2 2.2 %copy-start = (bf16[1,1,2,1024,1024]{4,3,2,1,0:T(8,128)(2,1)S(1)}, bf16[1,1,2,1024,1024]{4,3,2,1,0:T(8,128)(2,1)}, u32[]{:S(2)}) copy-start(bf16[1,1,2,1024,1024]{4,3,2,1,0:T(8,128)(2,1)} %lesser_ref.11) | copy-start | bytes 12582916
  16.4 4.5 %copy-start.13 = (f32[1,3]{1,0:T(1,128)S(1)}, f32[1,3]{1,0:T(1,128)}, u32[]{:S(2)}) copy-start(f32[1,3]{1,0:T(1,128)} %param.11) | copy-start | bytes 40
  17.2 0.8 copy-start.5
  18.3 23.6 %collective-permute-start.4 = (f32[2,1024]{1,0:T(2,128)S(1)}, f32[2,1024]{1,0:T(2,128)S(1)}, u32[]{:S(2)}, u32[]{:S(2)}) collective-permute-start(f32[2,1024]{1,0:T(2,128)S(1)} %get-tuple-element.34), channel_id=1, source_target_pairs={{4,12},{24,16},{5,13},{25,17},{6,14},{26,18},{7,15},{27,19}} | collective-permute-start | bytes 24584 | tf_op jit(solution)/shard_map/ppermute | solution.py:323
  18.9 22.9 %collective-permute-start.5 = (f32[2,1024]{1,0:T(2,128)S(1)}, f32[2,1024]{1,0:T(2,128)S(1)}, u32[]{:S(2)}, u32[]{:S(2)}) collective-permute-start(f32[2,1024]{1,0:T(2,128)S(1)} %get-tuple-element.36), channel_id=1, source_target_pairs={{4,20},{24,8},{5,21},{25,9},{6,22},{26,10},{7,23},{27,11}} | collective-permute-start | bytes 24584 | tf_op jit(solution)/shard_map/ppermute | solution.py:323
  19.6 22.3 %collective-permute-start.6 = (f32[2,1024]{1,0:T(2,128)S(1)}, f32[2,1024]{1,0:T(2,128)S(1)}, u32[]{:S(2)}, u32[]{:S(2)}) collective-permute-start(f32[2,1024]{1,0:T(2,128)S(1)} %get-tuple-element.35), channel_id=1, source_target_pairs={{4,28},{24,0},{5,29},{25,1},{6,30},{26,2},{7,31},{27,3}} | collective-permute-start | bytes 24584 | tf_op jit(solution)/shard_map/ppermute | solution.py:323
  21.5 2.2 %copy-start.1 = (bf16[1,1,2,1024,1024]{4,3,2,1,0:T(8,128)(2,1)S(1)}, bf16[1,1,2,1024,1024]{4,3,2,1,0:T(8,128)(2,1)}, u32[]{:S(2)}) copy-start(bf16[1,1,2,1024,1024]{4,3,2,1,0:T(8,128)(2,1)} %lesser_ref.11) | copy-start | bytes 12582916
  26.1 1.3 copy-start.7
  29.9 0.7 copy-start.9
  34.4 41.0 %collective-permute-start.9 = (bf16[1024,256]{1,0:T(8,128)(2,1)}, bf16[1024,256]{1,0:T(8,128)(2,1)S(1)}, u32[]{:S(2)}, u32[]{:S(2)}) collective-permute-start(bf16[1024,256]{1,0:T(8,128)(2,1)} %copy-done.5), channel_id=1, source_target_pairs={{0,12},{8,20},{12,24},{16,4},{20,8},{28,16},{1,13},{9,21},{13,25},... | collective-permute-start | bytes 1572872 | tf_op jit(solution)/shard_map/ppermute | solution.py:319
  59.0 1.6 %copy-start.4 = (bf16[1024,1024]{1,0:T(8,128)(2,1)S(1)}, bf16[1024,1024]{1,0:T(8,128)(2,1)}, u32[]{:S(2)}) copy-start(bf16[1024,1024]{1,0:T(8,128)(2,1)} %copy-done.3) | copy-start | bytes 6291460
  60.6 6.7 %copy-start.8 = (bf16[1024,896]{1,0:T(8,128)(2,1)S(1)}, bf16[1024,896]{1,0:T(8,128)(2,1)}, u32[]{:S(2)}) copy-start(bf16[1024,896]{1,0:T(8,128)(2,1)} %copy-done.7) | copy-start | bytes 5505028
  60.6 8.0 %copy-start.10 = (bf16[1024,128]{1,0:T(8,128)(2,1)S(1)}, bf16[1024,128]{1,0:T(8,128)(2,1)}, u32[]{:S(2)}) copy-start(bf16[1024,128]{1,0:T(8,128)(2,1)} %copy-done.9) | copy-start | bytes 786436
  62.3 13.1 %copy-start.12 = (f32[1,1024]{1,0:T(1,128)S(1)}, f32[1,1024]{1,0:T(1,128)}, u32[]{:S(2)}) copy-start(f32[1,1024]{1,0:T(1,128)} %param.15) | copy-start | bytes 12292
  62.3 59.6 %collective-permute-start.16 = (bf16[1024,1024]{1,0:T(8,128)(2,1)S(1)}, bf16[1024,1024]{1,0:T(8,128)(2,1)S(1)}, u32[]{:S(2)}, u32[]{:S(2)}) collective-permute-start(bf16[1024,1024]{1,0:T(8,128)(2,1)S(1)} %either.1), channel_id=1, source_target_pairs={{12,0},{16,28},{0,16},{28,12},{13,1},{17,29},{1,17},{29,13},{14,2}... | collective-permute-start | bytes 6291464 | tf_op jit(solution)/shard_map/ppermute | solution.py:331
  67.2 82.9 %collective-permute-start.14 = (bf16[1024,896]{1,0:T(8,128)(2,1)S(1)}, bf16[1024,896]{1,0:T(8,128)(2,1)S(1)}, u32[]{:S(2)}, u32[]{:S(2)}) collective-permute-start(bf16[1024,896]{1,0:T(8,128)(2,1)S(1)} %copy-done.8), channel_id=1, source_target_pairs={{4,16},{12,0},{16,28},{24,12},{5,17},{13,1},{17,29},{25,13},{6,18}... | collective-permute-start | bytes 5505032 | tf_op jit(solution)/shard_map/ppermute | solution.py:332
  68.6 8.2 %collective-permute-start.10 = (bf16[1024,128]{1,0:T(8,128)(2,1)S(1)}, bf16[1024,128]{1,0:T(8,128)(2,1)S(1)}, u32[]{:S(2)}, u32[]{:S(2)}) collective-permute-start(bf16[1024,128]{1,0:T(8,128)(2,1)S(1)} %copy-done.10), channel_id=1, source_target_pairs={{12,8},{16,20},{13,9},{17,21},{14,10},{18,22},{15,11},{19,23}} | collective-permute-start | bytes 786440 | tf_op jit(solution)/shard_map/ppermute | solution.py:334
  69.2 79.5 %collective-permute-start.15 = (bf16[1024,640]{1,0:T(8,128)(2,1)S(1)}, bf16[1024,640]{1,0:T(8,128)(2,1)S(1)}, u32[]{:S(2)}, u32[]{:S(2)}) collective-permute-start(bf16[1024,640]{1,0:T(8,128)(2,1)S(1)} %left.7.refs_3_), channel_id=1, source_target_pairs={{0,12},{8,20},{12,24},{16,4},{20,8},{28,16},{1,13},{9,21},{13,25},... | collective-permute-start | bytes 3932168 | tf_op jit(solution)/shard_map/ppermute | solution.py:333
  75.5 45.7 %collective-permute-start.8 = (f32[2,1024]{1,0:T(2,128)S(1)}, f32[2,1024]{1,0:T(2,128)S(1)}, u32[]{:S(2)}, u32[]{:S(2)}) collective-permute-start(f32[2,1024]{1,0:T(2,128)S(1)} %held.2), channel_id=1, source_target_pairs={{1,0},{2,1},{3,2},{5,4},{6,5},{7,6},{9,8},{10,9},{11,10},{13,12},{... | collective-permute-start | bytes 24584 | tf_op jit(solution)/shard_map/ppermute | solution.py:33
  76.8 3.8 %collective-permute-start.7 = (f32[2,1024]{1,0:T(2,128)S(1)}, f32[2,1024]{1,0:T(2,128)S(1)}, u32[]{:S(2)}, u32[]{:S(2)}) collective-permute-start(f32[2,1024]{1,0:T(2,128)S(1)} %broadcast_multiply_fusion), channel_id=1, source_target_pairs={{0,1},{1,2},{2,3},{4,5},{5,6},{6,7},{8,9},{9,10},{10,11},{12,13},{... | collective-permute-start | bytes 24584 | tf_op jit(solution)/shard_map/ppermute | solution.py:33
  80.6 73.6 %collective-permute-start.11 = (bf16[1024,128]{1,0:T(8,128)(2,1)S(1)}, bf16[1024,128]{1,0:T(8,128)(2,1)S(1)}, u32[]{:S(2)}, u32[]{:S(2)}) collective-permute-start(bf16[1024,128]{1,0:T(8,128)(2,1)S(1)} %copy-done.10), channel_id=1, source_target_pairs={{0,12},{8,20},{12,24},{16,4},{20,8},{28,16},{1,13},{9,21},{13,25},... | collective-permute-start | bytes 786440 | tf_op jit(solution)/shard_map/ppermute | solution.py:339
  121.2 33.0 %collective-permute-start.12 = (bf16[1024,128]{1,0:T(8,128)(2,1)S(1)}, bf16[1024,128]{1,0:T(8,128)(2,1)S(1)}, u32[]{:S(2)}, u32[]{:S(2)}) collective-permute-start(bf16[1024,128]{1,0:T(8,128)(2,1)S(1)} %copy-done.10), channel_id=1, source_target_pairs={{4,16},{24,12},{5,17},{25,13},{6,18},{26,14},{7,19},{27,15}} | collective-permute-start | bytes 786440 | tf_op jit(solution)/shard_map/ppermute | solution.py:338
  121.9 32.3 %collective-permute-start.13 = (bf16[1024,128]{1,0:T(8,128)(2,1)S(1)}, bf16[1024,128]{1,0:T(8,128)(2,1)S(1)}, u32[]{:S(2)}, u32[]{:S(2)}) collective-permute-start(bf16[1024,128]{1,0:T(8,128)(2,1)S(1)} %collective-permute-done.10), channel_id=1, source_target_pairs={{8,0},{20,28},{9,1},{21,29},{10,2},{22,30},{11,3},{23,31}} | collective-permute-start | bytes 786440 | tf_op jit(solution)/shard_map/ppermute | solution.py:337
  124.0 26.1 %copy-start.6 = (bf16[1024,256]{1,0:T(8,128)(2,1)S(1)}, bf16[1024,256]{1,0:T(8,128)(2,1)}, u32[]{:S(2)}) copy-start(bf16[1024,256]{1,0:T(8,128)(2,1)} %copy-done.5) | copy-start | bytes 1572868
